TPU v7x, 256 devices: a whole 4x4x8 slice. The times are simulated.
256 devices in a mesh: tok: 16 (over y, x), head: 16 (over z, core).
Axes of the slice: x: 4, y: 4, z: 8, core: 2. Of those that a mesh axis runs over, the one named last changes fastest.
Arguments:
- queries: bfloat16 [2, 4096, 16, 512], P(None, 'tok', 'head'), may hold values from -6 to 6
- key_rows: bfloat16 [2, 4096, 16, 512], P(None, 'tok', 'head'), may hold values from -6 to 6
- value_rows: bfloat16 [2, 4096, 16, 512], P(None, 'tok', 'head'), may hold values from -6 to 6
- step_sizes: float32 [2, 4096, 16], P(None, 'tok', 'head'), may hold values from 0 to 1, as said below
- out_grads: bfloat16 [2, 4096, 16, 512], P(None, 'tok', 'head'), may hold values from -0.59765625 to 0.59765625
- first_saved: bfloat16 [2, 16, 512, 512], P(None, 'head'), may hold values from -64 to 64
- second_saved: bfloat16 [2, 16, 512, 512], P(None, 'head'), may hold values from -64 to 64
- third_saved: bfloat16 [2, 16, 512, 512], P(None, 'head'), may hold values from -64 to 64
Outputs:
- query_grads: float32 [2, 4096, 16, 512], P(None, 'tok', 'head')
- key_grads: float32 [2, 4096, 16, 512], P(None, 'tok', 'head')
- value_grads: float32 [2, 4096, 16, 512], P(None, 'tok', 'head')
Inputs may be any that keep to these rules, and one draw needn't show every extreme that they name: `step_sizes`: positive step sizes.
All inputs are finite; a program needn't handle non-finite values.
Results may differ from a plain program's by a relative error of at most 0.04.
Values may be sent and summed in bfloat16 or wider, within the bound.
A program may use at most 128 MiB of HBM per device.

v0:
```python
import jax
import jax.numpy as jnp
from jax import lax
from jax.sharding import PartitionSpec as P

epsilon = 1e-06


def as_sent(value):

    def short(part):
        return part.astype(jnp.bfloat16) if part.dtype == jnp.float32 else part

    return jax.tree.map(short, value)


def product(pattern, left_side, right_side):
    return jnp.einsum(pattern, left_side, right_side, preferred_element_type=jnp.float32)


def add_terms(first_terms, second_terms):
    return tuple((paired[0] + paired[1] for paired in zip(first_terms, second_terms)))


def column_norm(matrix):
    return jnp.sqrt(jnp.sum(matrix * matrix, axis=1) + epsilon)


def forward_terms(weights, key_vecs, value_vecs, step_vecs):
    first_weight, second_weight, third_weight = weights
    gate_in = product("thd,hdf->thf", key_vecs, first_weight)
    lift_in = product("thd,hdf->thf", key_vecs, third_weight)
    squash = jax.nn.sigmoid(gate_in)
    activated = gate_in * squash
    gated_hidden = (activated * lift_in).astype(jnp.bfloat16)
    targets = (step_vecs[..., None] * value_vecs.astype(jnp.float32)).astype(jnp.bfloat16)
    back_hidden = product("thd,hfd->thf", targets, second_weight)
    slopes = squash * (1.0 + gate_in * (1.0 - squash))
    grad_gate = (back_hidden * lift_in * slopes).astype(jnp.bfloat16)
    grad_lift = (back_hidden * activated).astype(jnp.bfloat16)
    return (
        gate_in,
        lift_in,
        squash,
        activated,
        gated_hidden,
        targets,
        back_hidden,
        slopes,
        grad_gate,
        grad_lift,
    )


def apply_back(matrices, query_vecs, grad_vecs):
    first_weight, second_weight, third_weight = matrices
    gate_in = product("thd,hdf->thf", query_vecs, first_weight)
    lift_in = product("thd,hdf->thf", query_vecs, third_weight)
    squash = jax.nn.sigmoid(gate_in)
    activated = gate_in * squash
    gated_hidden = (activated * lift_in).astype(jnp.bfloat16)
    back_hidden = product("thd,hfd->thf", grad_vecs, second_weight)
    slopes = squash * (1.0 + gate_in * (1.0 - squash))
    grad_gate = (back_hidden * lift_in * slopes).astype(jnp.bfloat16)
    grad_lift = (back_hidden * activated).astype(jnp.bfloat16)
    query_out = product("thf,hdf->thd", grad_gate, first_weight) + product(
        "thf,hdf->thd", grad_lift, third_weight
    )
    pieces = (
        product("tha,thb->hab", query_vecs, grad_gate),
        product("tha,thb->hab", gated_hidden, grad_vecs),
        product("tha,thb->hab", query_vecs, grad_lift),
    )
    return (query_out, pieces)


def update_back(weights, key_vecs, step_vecs, forward, moves):
    first_weight, second_weight, third_weight = weights
    (
        gate_in,
        lift_in,
        squash,
        activated,
        gated_hidden,
        targets,
        back_hidden,
        slopes,
        grad_gate,
        grad_lift,
    ) = forward
    first_move, second_move, third_move = moves
    gated_back = product("thd,hfd->thf", targets, second_move)
    target_back = product("thf,hfd->thd", gated_hidden, second_move)
    first_back = product("thd,hdf->thf", key_vecs, first_move)
    third_back = product("thd,hdf->thf", key_vecs, third_move)
    curves = squash * (1.0 - squash) * (2.0 + gate_in * (1.0 - 2.0 * squash))
    hidden_back = (first_back * lift_in * slopes + third_back * activated).astype(jnp.bfloat16)
    gate_back = (
        (gated_back * lift_in + third_back * back_hidden) * slopes
        + first_back * back_hidden * lift_in * curves
    ).astype(jnp.bfloat16)
    lift_back = (first_back * back_hidden * slopes + gated_back * activated).astype(jnp.bfloat16)
    target_back = target_back + product("thf,hfd->thd", hidden_back, second_weight)
    value_out = step_vecs[..., None] * target_back
    key_out = (
        product("thf,hdf->thd", grad_gate, first_move)
        + product("thf,hdf->thd", grad_lift, third_move)
        + product("thf,hdf->thd", gate_back, first_weight)
        + product("thf,hdf->thd", lift_back, third_weight)
    )
    return (key_out, value_out, (gate_back, hidden_back, lift_back))


def start_terms(key_vecs, forward, backs):
    gate_back, hidden_back, lift_back = backs
    return (
        product("tha,thb->hab", key_vecs, gate_back),
        product("tha,thb->hab", hidden_back, forward[5]),
        product("tha,thb->hab", key_vecs, lift_back),
    )


def renorm_terms(cotangents, matrices, weights, kept_norms, summed_norms, inner_sums):
    moves = []
    direct = []
    for cotangent, matrix, weight, kept, summed, inner in zip(
        cotangents, matrices, weights, kept_norms, summed_norms, inner_sums
    ):
        factor = kept / summed
        moves.append(
            cotangent * factor[:, None, :]
            - matrix * (factor * inner / (summed * summed))[:, None, :]
        )
        direct.append(weight.astype(jnp.float32) * (inner / (summed * kept))[:, None, :])
    return (tuple(moves), tuple(direct))


def local(
    queries, key_rows, value_rows, step_sizes, out_grads, first_saved, second_saved, third_saved
):
    tok_count = lax.axis_size("tok")
    position = lax.axis_index("tok")

    def own_rows(matrix):
        row_count = matrix.shape[1] // tok_count
        return lax.dynamic_slice_in_dim(matrix, position * row_count, row_count, 1)

    def column_total(values):
        return lax.psum(values, "tok")

    def rows_whole(values):
        return jax.tree.map(
            lambda part, own: part.astype(own.dtype),
            lax.all_gather(as_sent(values), "tok", axis=1, tiled=True),
            values,
        )

    def cotangent_rows(values):
        return (
            lax.psum_scatter(
                values[0].astype(jnp.bfloat16), "tok", scatter_dimension=1, tiled=True
            ).astype(jnp.float32),
            lax.psum_scatter(
                values[1].astype(jnp.bfloat16), "tok", scatter_dimension=1, tiled=True
            ).astype(jnp.float32),
            lax.psum_scatter(
                values[2].astype(jnp.bfloat16), "tok", scatter_dimension=1, tiled=True
            ).astype(jnp.float32),
        )

    def restate(weights, key_vecs, value_vecs, step_vecs, need_whole):
        forward = forward_terms(weights, key_vecs, value_vecs, step_vecs)
        pieces = (
            product("tha,thb->hab", key_vecs, forward[8]),
            product("tha,thb->hab", forward[4], forward[5]),
            product("tha,thb->hab", key_vecs, forward[9]),
        )
        kept_norms = tuple((column_norm(weight.astype(jnp.float32)) for weight in weights))
        changes = (
            lax.psum(pieces[0].astype(jnp.bfloat16), "tok").astype(jnp.float32),
            lax.psum(pieces[1].astype(jnp.bfloat16), "tok").astype(jnp.float32),
            lax.psum(pieces[2].astype(jnp.bfloat16), "tok").astype(jnp.float32),
        )
        matrices = tuple(
            (weight.astype(jnp.float32) + change for weight, change in zip(weights, changes))
        )
        summed_norms = tuple((column_norm(matrix) for matrix in matrices))
        applied = (
            tuple(
                (
                    (matrix * (kept / summed)[:, None, :]).astype(jnp.bfloat16)
                    for matrix, kept, summed in zip(matrices, kept_norms, summed_norms)
                )
            )
            if need_whole
            else None
        )
        matrix_rows = tuple((own_rows(matrix) for matrix in matrices))
        return (forward, matrix_rows, kept_norms, summed_norms, applied)

    def renorm_back(cotangents, matrix_rows, weights, kept_norms, summed_norms):
        inner_sums = column_total(
            tuple(
                (
                    jnp.sum(cotangent * matrix, axis=1)
                    for cotangent, matrix in zip(cotangents, matrix_rows)
                )
            )
        )
        return renorm_terms(
            cotangents,
            matrix_rows,
            tuple((own_rows(weight) for weight in weights)),
            kept_norms,
            summed_norms,
            inner_sums,
        )

    later = (first_saved[1], second_saved[1], third_saved[1])
    earlier = (first_saved[0], second_saved[0], third_saved[0])
    forward_late, rows_late, kept_late, summed_late, applied_late = restate(
        later, key_rows[1], value_rows[1], step_sizes[1], True
    )
    query_late, pieces_late = apply_back(applied_late, queries[1], out_grads[1])
    cot_late = cotangent_rows(pieces_late)
    moves_late, direct_late = renorm_back(cot_late, rows_late, later, kept_late, summed_late)
    whole_late = rows_whole(tuple((move.astype(jnp.bfloat16) for move in moves_late)))
    key_late, value_late, backs_late = update_back(
        later, key_rows[1], step_sizes[1], forward_late, whole_late
    )
    starts_late = start_terms(key_rows[1], forward_late, backs_late)
    query_early, pieces_early = apply_back(later, queries[0], out_grads[0])
    summed_cot = add_terms(cotangent_rows(pieces_early), cotangent_rows(starts_late))
    state_cot = add_terms(add_terms(summed_cot, moves_late), direct_late)
    forward_early, rows_early, kept_early, summed_early, unused_new = restate(
        earlier, key_rows[0], value_rows[0], step_sizes[0], False
    )
    moves_early, unused_direct = renorm_back(
        state_cot, rows_early, earlier, kept_early, summed_early
    )
    whole_early = rows_whole(tuple((move.astype(jnp.bfloat16) for move in moves_early)))
    key_early, value_early, unused_backs = update_back(
        earlier, key_rows[0], step_sizes[0], forward_early, whole_early
    )
    return (
        jnp.stack([query_early, query_late]),
        jnp.stack([key_early, key_late]),
        jnp.stack([value_early, value_late]),
    )


def solution(mesh):
    placed = (
        P(None, "tok", "head", None),
        P(None, "tok", "head", None),
        P(None, "tok", "head", None),
        P(None, "tok", "head"),
        P(None, "tok", "head", None),
        P(None, "head", None, None),
        P(None, "head", None, None),
        P(None, "head", None, None),
    )
    return jax.shard_map(
        local,
        mesh=mesh,
        in_specs=placed,
        out_specs=(
            P(None, "tok", "head", None),
            P(None, "tok", "head", None),
            P(None, "tok", "head", None),
        ),
        check_vma=False,
    )
```

profile of v0, /device:TPU:2, one launch (start us, length us, event | category | flops | bytes accessed | tf_op | source)
XLA Modules:
  0.0 786.4 jit_solution(11410710101102461298)
XLA Ops:
  7.2 1.6 convolution_bitcast_fusion.18
  8.8 1.6 convolution_bitcast_fusion.9
  13.4 1.1 fusion
  15.8 1.1 fusion.8
  16.9 1.2 fusion.1
  18.1 1.2 fusion.14
  19.3 1.2 fusion.2
  20.4 1.1 fusion.11
  21.7 109.0 %all-reduce.19.cloned.1.call-done = (bf16[1,512,512]{2,1,0:T(8,128)(2,1)}, bf16[1,512,512]{2,1,0:T(8,128)(2,1)}, bf16[1,512,512]{2,1,0:T(8,128)(2,1)}, bf16[1,51...) async-done(((bf16[1,512,512]{2,1,0:T(8,128)(2,1)}, bf16[1,512,512]{2,1,0:T(8,128)(2,1)}, bf16[1,512,512]{2,1,0:T(8,128)(2,1)}, ...) | async-done | bytes 3145744 | tf_op jit(solution)/shard_map/psum | solution.py:180
  130.7 5.0 fusion.34
  138.5 2.4 fusion.36
  141.5 1.2 fusion.104
  143.4 1.1 fusion.6
  144.5 3.6 copy.70
  148.0 2.1 fusion.5
  150.1 3.6 copy.68
  153.7 2.4 fusion.4
  158.2 1.1 fusion.12
  159.4 2.5 fusion.100
  161.9 1.1 fusion.79
  163.1 1.1 fusion.3
  164.2 2.3 fusion.30
  168.5 85.4 %all-reduce.17.cloned.1.call-done = (bf16[1,512,512]{2,0,1:T(2,128)(2,1)}, bf16[1,512,512]{2,0,1:T(2,128)(2,1)}) async-done(((bf16[1,512,512]{2,0,1:T(2,128)(2,1)}, bf16[1,512,512]{2,0,1:T(2,128)(2,1)}), (bf16[1,512,512]{2,0,1:T(2,128)(2,1)}, bf16[1,512,512]{2,0,1:T(2,128)(2,1)})) %all-reduce.17.cloned.1.call-update) | async-done | bytes 1048592
  253.9 0.9 constant_dynamic-slice_fusion.3
  254.8 0.9 constant_dynamic-slice_fusion.4
  257.4 77.2 %reduce-scatter.4.cloned.1.call-done = bf16[1,32,512]{2,1,0:T(8,128)(2,1)} async-done(((bf16[1,512,512]{2,1,0:T(8,128)(2,1)}), bf16[1,32,512]{2,1,0:T(8,128)(2,1)}) %reduce-scatter.4.cloned.1.call-update) | async-done | bytes 32784 | tf_op jit(solution)/shard_map/reduce_scatter | solution.py:163
  334.7 0.9 fusion.183
  335.5 37.4 %all-reduce.7 = (f32[1,512]{1,0:T(1,128)}, f32[1,512]{1,0:T(1,128)S(1)}, f32[1,512]{1,0:T(1,128)}) all-reduce(f32[1,512]{1,0:T(1,128)S(1)} %bitcast.593, f32[1,512]{1,0:T(1,128)S(1)} %bitcast.585, f32[1,512]{1,0:T(1,128)S(1)} %bitcast.586), channel_id=1, replica_groups=mesh['tok'=16,'head'=16] {'tok'}, use_global_device_ids=true, to_apply=%region_12.0 | all-reduce | flops 1536 | bytes 12288 | tf_op jit(solution)/shard_map/psum | solution.py:149
  375.7 23.6 %all_gather.20 = bf16[1,512,512]{2,1,0:T(8,128)(2,1)S(1)} all-gather(bf16[1,32,512]{2,1,0:T(8,128)(2,1)S(1)} %fusion.199), channel_id=1, replica_groups=mesh['tok'=16,'head'=16] {'tok'}, dimensions={1}, use_global_device_ids=true | all-gather | bytes 557056 | tf_op jit(solution)/shard_map/all_gather | solution.py:154
  403.6 21.8 %all_gather.18 = bf16[1,512,512]{2,1,0:T(8,128)(2,1)S(1)} all-gather(bf16[1,32,512]{2,1,0:T(8,128)(2,1)S(1)} %fusion.201), channel_id=1, replica_groups=mesh['tok'=16,'head'=16] {'tok'}, dimensions={1}, use_global_device_ids=true | all-gather | bytes 557056 | tf_op jit(solution)/shard_map/all_gather | solution.py:154
  425.4 23.8 %all_gather.19 = bf16[1,512,512]{2,1,0:T(8,128)(2,1)S(1)} all-gather(bf16[1,32,512]{2,1,0:T(8,128)(2,1)S(1)} %fusion.200), channel_id=1, replica_groups=mesh['tok'=16,'head'=16] {'tok'}, dimensions={1}, use_global_device_ids=true | all-gather | bytes 557056 | tf_op jit(solution)/shard_map/all_gather | solution.py:154
  451.7 1.5 fusion.112
  453.9 1.2 fusion.13
  455.1 2.1 fusion.9
  457.3 3.6 copy.66
  460.8 3.6 copy.76
  464.4 1.6 fusion.130
  466.0 1.2 fusion.29
  468.4 1.1 fusion.7
  469.6 3.6 copy.72
  473.2 2.0 fusion.10
  475.2 3.6 copy.78
  478.8 1.3 pad_maximum_fusion
  480.2 2.0 copy.87
  484.4 1.1 fusion.22
  488.6 1.1 fusion.28
  489.7 41.9 %reduce-scatter.8.cloned.1.call-done = bf16[1,32,512]{2,1,0:T(8,128)(2,1)} async-done(((bf16[1,512,512]{2,1,0:T(8,128)(2,1)}), bf16[1,32,512]{2,1,0:T(8,128)(2,1)}) %reduce-scatter.8.cloned.1.call-update) | async-done | bytes 32784 | tf_op jit(solution)/shard_map/reduce_scatter | solution.py:163
  531.6 2.1 multiply_reduce_fusion.6
  533.8 115.2 %all-reduce.15.cloned.1.call-done = (bf16[1,512,512]{2,0,1:T(2,128)(2,1)}, bf16[1,512,512]{2,0,1:T(2,128)(2,1)}, bf16[1,512,512]{2,0,1:T(2,128)(2,1)}, bf16[1,512,512]{2,0,1:T(2,128)(2,1)}) async-done(((bf16[1,512,512]{2,0,1:T(2,128)(2,1)}, bf16[1,512,512]{2,0,1:T(2,128)(2,1)}, bf16[1,512,512]{2,0,1:T(2,128)(2,1)}, bf16[1,512,512]{2,0,1:T(2,128)(2,1)}), (bf16[1,512,512]{2,0,1:T(2,128)(2,1)}, ...) | async-done | bytes 2097168
  649.0 0.9 constant_dynamic-slice_fusion.2
  649.9 0.9 constant_dynamic-slice_fusion.5
  650.8 0.9 constant_dynamic-slice_fusion
  651.7 0.9 constant_dynamic-slice_fusion.1
  652.6 0.9 multiply_reduce_fusion.8
  654.3 0.9 multiply_reduce_fusion.7
  655.9 36.5 %all-reduce.6 = (f32[1,512]{1,0:T(1,128)S(1)}, f32[1,512]{1,0:T(1,128)S(1)}, f32[1,512]{1,0:T(1,128)S(1)}) all-reduce(f32[1,512]{1,0:T(1,128)S(1)} %bitcast.582, f32[1,512]{1,0:T(1,128)S(1)} %bitcast.583, f32[1,512]{1,0:T(1,128)S(1)} %bitcast.584), channel_id=1, replica_groups=mesh['tok'=16,'head'=16] {'tok'}, use_global_device_ids=true, to_apply=%region_38.0 | all-reduce | flops 1536 | bytes 12288 | tf_op jit(solution)/shard_map/psum | solution.py:149
  694.0 23.8 %all_gather.21 = bf16[1,512,512]{2,1,0:T(8,128)(2,1)S(1)} all-gather(bf16[1,32,512]{2,1,0:T(8,128)(2,1)S(1)} %subtract_convert_fusion.2), channel_id=1, replica_groups=mesh['tok'=16,'head'=16] {'tok'}, dimensions={1}, use_global_device_ids=true | all-gather | bytes 557056 | tf_op jit(solution)/shard_map/all_gather | solution.py:154
  720.5 21.7 %all_gather.23 = bf16[1,512,512]{2,1,0:T(8,128)(2,1)S(1)} all-gather(bf16[1,32,512]{2,1,0:T(8,128)(2,1)S(1)} %subtract_convert_fusion), channel_id=1, replica_groups=mesh['tok'=16,'head'=16] {'tok'}, dimensions={1}, use_global_device_ids=true | all-gather | bytes 557056 | tf_op jit(solution)/shard_map/all_gather | solution.py:154
  742.6 1.1 fusion.55
  745.3 23.6 %all_gather.22 = bf16[1,512,512]{2,1,0:T(8,128)(2,1)S(1)} all-gather(bf16[1,32,512]{2,1,0:T(8,128)(2,1)S(1)} %subtract_convert_fusion.1), channel_id=1, replica_groups=mesh['tok'=16,'head'=16] {'tok'}, dimensions={1}, use_global_device_ids=true | all-gather | bytes 557056 | tf_op jit(solution)/shard_map/all_gather | solution.py:154
  770.2 1.1 copy-done.2
  773.6 1.9 copy.88
  775.5 2.0 fusion.18
  777.6 1.9 copy.89
  (259 shorter events, 41.2 us)
Async XLA Ops:
  7.2 1.6 copy-start
  7.2 3.2 copy-start.1
  7.2 123.5 %all-reduce.19.cloned.1.call-start = ((), (), s32[]{:S(2)}) async-start(), calls=%async_computation.8 | async-start | bytes 6291456 | tf_op jit(solution)/shard_map/psum | solution.py:180
  8.8 3.8 copy-start.35
  10.4 4.5 copy-start.30
  10.4 1.6 copy-start.7
  10.8 1.8 copy-start.37
  10.8 1.4 copy-start.11
  11.8 3.2 copy-start.33
  11.8 6.3 copy-start.69
  13.4 3.5 copy-start.14
  13.4 5.9 copy-start.20
  15.8 4.7 copy-start.16
  21.6 109.1 %copy-start.3 = (bf16[2,1,512,512]{3,2,1,0:T(8,128)(2,1)S(1)}, bf16[2,1,512,512]{3,2,1,0:T(8,128)(2,1)}, u32[]{:S(2)}) copy-start(bf16[2,1,512,512]{3,2,1,0:T(8,128)(2,1)} %param.13) | copy-start | bytes 3145732
  21.6 232.2 %all-reduce.17.cloned.1.call-start = ((), (), s32[]{:S(2)}) async-start(), calls=%async_computation.7 | async-start | bytes 4194304
  130.7 5.6 copy-start.6
  130.7 5.6 copy-start.28
  136.3 1.4 copy-start.56
  136.7 4.8 copy-start.95
  136.7 1.5 copy-start.8
  137.3 1.2 copy-start.55
  137.7 3.8 copy-start.96
  138.5 3.0 copy-start.92
  153.7 181.0 %reduce-scatter.4.cloned.1.call-start = ((), (), s32[]{:S(2)}) async-start(), calls=%async_computation.3 | async-start | bytes 557056 | tf_op jit(solution)/shard_map/reduce_scatter | solution.py:163
  156.2 333.5 %reduce-scatter.6.cloned.1.call-start = ((), (), s32[]{:S(2)}) async-start(), calls=%async_computation.4 | async-start | bytes 557056 | tf_op jit(solution)/shard_map/reduce_scatter | solution.py:163
  156.6 1.6 copy-start.93
  159.3 372.3 %reduce-scatter.8.cloned.1.call-start = ((), (), s32[]{:S(2)}) async-start(), calls=%async_computation.5 | async-start | bytes 557056 | tf_op jit(solution)/shard_map/reduce_scatter | solution.py:163
  375.7 23.6 %copy-start.91 = (f32[1,512]{1,0:T(1,128)S(1)}, f32[1,512]{1,0:T(1,128)}, u32[]{:S(2)}) copy-start(f32[1,512]{1,0:T(1,128)} %get-tuple-element.29) | copy-start | bytes 6148
  400.6 2.2 copy-start.57
  425.4 24.2 %copy-start.4 = (bf16[1,512,512]{2,1,0:T(8,128)(2,1)}, bf16[1,512,512]{2,1,0:T(8,128)(2,1)S(1)}, u32[]{:S(2)}) copy-start(bf16[1,512,512]{2,1,0:T(8,128)(2,1)S(1)} %all_gather.18) | copy-start | bytes 1572868
  449.2 1.6 copy-start.24
  449.2 1.2 copy-start.12
  449.2 1.6 copy-start.54
  450.5 1.2 copy-start.38
  455.1 193.9 %all-reduce.15.cloned.1.call-start = ((), (), s32[]{:S(2)}) async-start(), calls=%async_computation.6 | async-start | bytes 8388608
  464.4 1.6 copy-start.27
  464.4 1.6 copy-start.46
  466.0 1.2 copy-start.73
  466.0 2.5 copy-start.42
  480.1 2.1 copy-start.87
  480.1 2.1 copy-start.88
  480.1 2.7 copy-start.85
  480.1 2.7 copy-start.86
  480.1 3.3 copy-start.5
  480.1 3.3 copy-start.15
  482.2 1.6 copy-start.9
  484.4 1.1 copy-start.44
  488.5 43.1 %slice-start.2 = ((bf16[2,1,512,512]{3,2,1,0:T(8,128)(2,1)}), bf16[1,1,512,512]{3,2,1,0:T(8,128)(2,1)S(1)}, s32[]{:S(2)}) async-start(bf16[2,1,512,512]{3,2,1,0:T(8,128)(2,1)} %param.14), calls=%async_computation.11 | async-start | bytes 1048576 | tf_op jit(solution)/shard_map/slice | solution.py:219
  488.5 43.1 %copy-start.58 = (bf16[1,32,512]{2,1,0:T(8,128)(2,1)S(1)}, bf16[1,32,512]{2,1,0:T(8,128)(2,1)}, u32[]{:S(2)}) copy-start(bf16[1,32,512]{2,1,0:T(8,128)(2,1)} %reduce-scatter.4.cloned.1.call-done) | copy-start | bytes 98308
  488.5 43.1 %copy-start.65 = (f32[1,512]{1,0:T(1,128)S(1)}, f32[1,512]{1,0:T(1,128)}, u32[]{:S(2)}) copy-start(f32[1,512]{1,0:T(1,128)} %copy-done.64) | copy-start | bytes 6148
  488.6 43.1 %copy-start.75 = (f32[1,512]{1,0:T(1,128)S(1)}, f32[1,512]{1,0:T(1,128)}, u32[]{:S(2)}) copy-start(f32[1,512]{1,0:T(1,128)} %get-tuple-element.85) | copy-start | bytes 6148
  488.6 164.1 %copy-start.63 = (f32[1,512]{1,0:T(1,128)S(1)}, f32[1,512]{1,0:T(1,128)}, u32[]{:S(2)}) copy-start(f32[1,512]{1,0:T(1,128)} %copy-done.62) | copy-start | bytes 6148
  489.7 163.0 %slice-start.1 = ((bf16[2,1,512,512]{3,2,1,0:T(8,128)(2,1)}), bf16[1,1,512,512]{3,2,1,0:T(8,128)(2,1)S(1)}, s32[]{:S(2)}) async-start(bf16[2,1,512,512]{3,2,1,0:T(8,128)(2,1)} %param.13), calls=%async_computation.10 | async-start | bytes 1048576 | tf_op jit(solution)/shard_map/slice | solution.py:219
  533.7 119.9 %slice-start = ((bf16[2,1,512,512]{3,2,1,0:T(8,128)(2,1)}), bf16[1,1,512,512]{3,2,1,0:T(8,128)(2,1)S(1)}, s32[]{:S(2)}) async-start(bf16[2,1,512,512]{3,2,1,0:T(8,128)(2,1)} %param.15), calls=%async_computation.9 | async-start | bytes 1048576 | tf_op jit(solution)/shard_map/slice | solution.py:219
  718.7 53.3 %copy-start.47 = (f32[256,1,512]{0,2,1:T(8,128)}, f32[256,1,512]{0,2,1:T(8,128)S(1)}, u32[]{:S(2)}) copy-start(f32[256,1,512]{0,2,1:T(8,128)S(1)} %convolution_bitcast_fusion.6) | copy-start | bytes 1572868
  719.1 23.1 %copy-start.13 = (bf16[2,256,1,512]{3,1,2,0:T(8,128)(2,1)S(1)}, bf16[2,256,1,512]{3,1,2,0:T(8,128)(2,1)}, u32[]{:S(2)}) copy-start(bf16[2,256,1,512]{3,1,2,0:T(8,128)(2,1)} %param.10) | copy-start | bytes 1572868
  720.5 21.7 %copy-start.70 = (f32[1,256,1]{1,2,0:T(1,128)S(1)}, f32[1,256,1]{1,2,0:T(1,128)}, u32[]{:S(2)}) copy-start(f32[1,256,1]{1,2,0:T(1,128)} %copy-done.69) | copy-start | bytes 3076
  768.9 1.3 copy-start.52
  769.9 2.1 copy-start.48
  769.9 1.5 copy-start.2
  769.9 1.6 copy-start.31
  773.6 1.9 copy-start.10
  773.6 1.9 copy-start.32
  775.5 2.0 copy-start.29
  (42 other events, 34.5 us)
Sparse Core Ops, SparseCore 0:
  21.7 108.8 all-reduce.18
  153.8 99.9 all-reduce.16
  257.7 76.8 reduce-scatter.3
  338.0 76.6 reduce-scatter.5
  455.2 76.3 reduce-scatter.7
  535.1 113.8 all-reduce.14
where the time goes:
time: 789 us; the launch traced here: 786 us
  waiting for transfers between devices  429 us (54%)
  blocking collectives  212 us (27%)
  local copies, waits for them, and re-layouts  53.8 us (7%)
  matrix products  48.8 us (6%)
  other arithmetic  26.7 us (3%)
  between operations  15.7 us (2%)
    unnamed x8, waiting for transfers between devices  201 us
    all_gather x6, blocking collectives, rows_whole(): lax.all_gather(as_sent(values), 'tok', axis=1, tiled=True)  138 us
    reduce_scatter x3, waiting for transfers between devices, cotangent_rows(): lax.psum_scatter(values[1].astype(jnp.bfloat16), 'tok', scatter_dimension...  119 us
    psum x1, waiting for transfers between devices, restate(): lax.psum(pieces[0].astype(jnp.bfloat16), 'tok').astype(jnp.float32)  109 us
    psum x2, blocking collectives, column_total(): return lax.psum(values, 'tok')  74 us
    dot_general x49, matrix products, product(): jnp.einsum(pattern, left_side, right_side, preferred_element_type=jnp.flo...  48.8 us
    unnamed x204, local copies, waits for them, and re-layouts  32.4 us
  transfers between devices with their start and end apart: 6, of which 5 were waited for; matrix products, arithmetic and copies ran while one was open for 7% of the time, Pallas kernels for 0%

commit v1 on v0

v1 whole, which is shorter than its diff:
```python
import functools

import jax
import jax.numpy as jnp
from jax import lax
from jax.experimental import pallas as pl
from jax.experimental.pallas import tpu as pltpu
from jax.sharding import PartitionSpec as P

EPSILON = 1e-06
MESH = pl.DeviceIdType.MESH
F32, BF16 = jnp.float32, jnp.bfloat16
SIDE = 4
TOK, DIM = 256, 512
HALF = DIM // 2
BAND = HALF // SIDE
OWN = BAND // SIDE
CHUNK = 16
D_LATE, C_LATE, C_EARLY, D_EARLY = range(4)
R_LATE, M_LATE, M_EARLY = range(3)


def nn(left, right):
    return lax.dot_general(left, right, (((1,), (0,)), ((), ())), preferred_element_type=F32)


def nt(left, right):
    return lax.dot_general(left, right, (((1,), (1,)), ((), ())), preferred_element_type=F32)


def tn(left, right):
    return lax.dot_general(left, right, (((0,), (0,)), ((), ())), preferred_element_type=F32)


def kernel(
    q_any, k_any, v_any, s_any, g_any, w1_any, w2_any, w3_any,
    query_any, key_any, value_any,
    q, k, v, s, g, w,
    a_in, b_in, back, squash, gated, target, ga, gb,
    a_out, b_out, back_out, gated_out, ga_out, gb_out,
    first_back, third_back, gated_back, gate_back, hidden_back, lift_back,
    c_early, own_w, own_p, own_add, kept, summed,
    snd, got1, mid, got2, whole, out,
    in_sem, out_sem,
    rs1_send, rs1_recv, rs2_send, rs2_recv, ag1_send, ag1_recv, ag2_send, ag2_recv,
):
    tok = lax.axis_index("tok")
    x, y = lax.rem(tok, SIDE), tok // SIDE
    along_x = [(y * SIDE + lax.rem(x + d, SIDE), lax.rem(x + d, SIDE)) for d in range(1, SIDE)]
    along_y = [(lax.rem(y + d, SIDE) * SIDE + x, lax.rem(y + d, SIDE)) for d in range(1, SIDE)]

    weights_any = (w1_any, w2_any, w3_any)
    loads = {}

    def load(name, source, place):
        copy = pltpu.make_async_copy(source, place, in_sem.at[len(loads)])
        copy.start()
        loads[name] = copy

    def arrived(*names):
        for name in names:
            loads[name].wait()

    load("s", s_any, s)
    for b in (1, 0):
        load(("k", b), k_any.at[b], k.at[b])
        load(("w", b, 0), weights_any[0].at[b], w.at[b, 0])
        load(("w", b, 2), weights_any[2].at[b], w.at[b, 2])
        load(("v", b), v_any.at[b], v.at[b])
        load(("w", b, 1), weights_any[1].at[b], w.at[b, 1])
    for b in (0, 1):
        load(("q", b), q_any.at[b], q.at[b])
        load(("g", b), g_any.at[b], g.at[b])

    barrier = pltpu.get_barrier_semaphore()
    for peer, _ in along_x + along_y:
        pl.semaphore_signal(barrier, inc=1, device_id={"tok": peer}, device_id_type=MESH)

    started = {}

    def send(name, source, place, send_sem, recv_sem, peer):
        copy = pltpu.make_async_remote_copy(
            src_ref=source, dst_ref=place, send_sem=send_sem, recv_sem=recv_sem,
            device_id={"tok": peer}, device_id_type=MESH,
        )
        copy.start()
        started.setdefault(name, []).append(copy)

    def received(name):
        for copy in started[name]:
            copy.wait_recv()

    def rows(start, size):
        return pl.ds(pl.multiple_of(start, OWN), size)

    def rs_start(c, m):
        for d in range(SIDE - 1):
            for half, (peer, at) in ((0, along_x[d]), (1, along_y[d])):
                send(("rs1", c, m, half), snd.at[c, m, rows(half * HALF + at * BAND, BAND)], got1.at[c, m, half, d],
                     rs1_send.at[c, m, half, d], rs1_recv.at[c, m, half, d], peer)

    def rs_middle(c, m):
        for half, mine, peers in ((0, x, along_y), (1, y, along_x)):
            received(("rs1", c, m, half))
            total = snd[c, m, rows(half * HALF + mine * BAND, BAND), :].astype(F32)
            for d in range(SIDE - 1):
                total = total + got1[c, m, half, d].astype(F32)
            mid[c, m, half] = total.astype(BF16)
            for d, (peer, at) in enumerate(peers):
                send(("rs2", c, m, half), mid.at[c, m, half, rows(at * OWN, OWN)], got2.at[c, m, half, d],
                     rs2_send.at[c, m, half, d], rs2_recv.at[c, m, half, d], peer)

    def rs_end(c, m):
        parts = []
        for half, mine in ((0, y), (1, x)):
            received(("rs2", c, m, half))
            total = mid[c, m, half, rows(mine * OWN, OWN), :].astype(F32)
            for d in range(SIDE - 1):
                total = total + got2[c, m, half, d].astype(F32)
            parts.append(total)
        return jnp.concatenate(parts, axis=0)

    own_rows = (x * BAND + y * OWN, HALF + y * BAND + x * OWN)
    band_rows = (x * BAND, HALF + y * BAND)

    def ag_start(c, m, value):
        for half, peers in ((0, along_y), (1, along_x)):
            whole[c, m, rows(own_rows[half], OWN), :] = value[half * OWN:(half + 1) * OWN]
            for d, (peer, _) in enumerate(peers):
                place = whole.at[c, m, rows(own_rows[half], OWN)]
                send(("ag1", c, m, half), place, place, ag1_send.at[c, m, half, d], ag1_recv.at[c, m, half, d], peer)

    def ag_middle(c, m):
        for half, peers in ((0, along_x), (1, along_y)):
            received(("ag1", c, m, half))
            for d, (peer, _) in enumerate(peers):
                place = whole.at[c, m, rows(band_rows[half], BAND)]
                send(("ag2", c, m, half), place, place, ag2_send.at[c, m, half, d], ag2_recv.at[c, m, half, d], peer)

    def ag_end(c, m):
        for half in (0, 1):
            received(("ag2", c, m, half))

    def by_chunk(step):
        def body(i, carry):
            step(rows(i * CHUNK, CHUNK))
            return carry

        lax.fori_loop(0, TOK // CHUNK, body, 0)

    def forward_inner(b):
        a_in[b] = nn(k[b], w[b, 0])
        b_in[b] = nn(k[b], w[b, 2])

    def forward_target(b):
        step = jnp.broadcast_to(s[b], (128, TOK)).T
        for j in range(DIM // 128):
            lanes = slice(j * 128, (j + 1) * 128)
            target[b, :, lanes] = (step * v[b, :, lanes].astype(F32)).astype(BF16)

    def forward_rest(b):
        back[b] = nt(target[b], w[b, 1])

        def step(r):
            gate, lift, hidden = a_in[b, r, :], b_in[b, r, :], back[b, r, :]
            sg = jax.nn.sigmoid(gate)
            activated = gate * sg
            slope = sg * (1.0 + gate * (1.0 - sg))
            squash[b, r, :] = sg
            gated[b, r, :] = (activated * lift).astype(BF16)
            ga[b, r, :] = (hidden * lift * slope).astype(BF16)
            gb[b, r, :] = (hidden * activated).astype(BF16)

        by_chunk(step)

    def update_term(b, m):
        if m == 0:
            return tn(ga[b], k[b])
        if m == 1:
            return tn(target[b], gated[b])
        return tn(gb[b], k[b])

    row_of = lax.broadcasted_iota(jnp.int32, (2 * OWN, DIM), 0)
    col_of = lax.broadcasted_iota(jnp.int32, (2 * OWN, DIM), 1)
    wanted = jnp.where(row_of < OWN, own_rows[0] + row_of, own_rows[1] + row_of - OWN)
    picker = jnp.where(col_of == wanted, 1.0, 0.0).astype(BF16)

    def own_columns(b, m):
        mine = nt(picker, w[b, m])
        own_w[b, m] = mine
        kept[b, m] = jnp.broadcast_to(jnp.sqrt(jnp.sum(mine * mine, axis=1, keepdims=True) + EPSILON), (2 * OWN, 128))

    def own_update(b, m, change):
        total = own_w[b, m] + change
        own_p[b, m] = total
        summed[b, m] = jnp.broadcast_to(jnp.sqrt(jnp.sum(total * total, axis=1, keepdims=True) + EPSILON), (2 * OWN, 128))
        return total * (kept[b, m, :, :1] / summed[b, m, :, :1])

    def renorm_back(b, m, cotangent):
        matrix, before, after = own_p[b, m], kept[b, m, :, :1], summed[b, m, :, :1]
        inner = jnp.sum(cotangent * matrix, axis=1, keepdims=True)
        factor = before / after
        move = cotangent * factor - matrix * (factor * inner / (after * after))
        return move, own_w[b, m] * (inner / (after * before))

    def output_step():
        def step(r):
            gate, lift, hidden = a_out[r, :], b_out[r, :], back_out[r, :]
            sg = jax.nn.sigmoid(gate)
            activated = gate * sg
            slope = sg * (1.0 + gate * (1.0 - sg))
            gated_out[r, :] = (activated * lift).astype(BF16)
            ga_out[r, :] = (hidden * lift * slope).astype(BF16)
            gb_out[r, :] = (hidden * activated).astype(BF16)

        by_chunk(step)

    def store_out(i, b, value):
        for j in range(DIM // 128):
            out[i, pl.ds(b * TOK * 4 + j, TOK, stride=4), :] = value[:, j * 128:(j + 1) * 128]
        place = pl.ds(b * TOK * 4, TOK * 4)
        target_any = (query_any, key_any, value_any)[i]
        copy = pltpu.make_async_copy(out.at[i, place], target_any.at[place], out_sem.at[i, b])
        copy.start()
        return copy

    stores = []

    def update_step(b):
        def step(r):
            gate, lift, hidden, sg = a_in[b, r, :], b_in[b, r, :], back[b, r, :], squash[b, r, :]
            fb, tb, gdb = first_back[r, :], third_back[r, :], gated_back[r, :]
            activated = gate * sg
            rest = 1.0 - sg
            slope = sg * (1.0 + gate * rest)
            curve = sg * rest * (2.0 + gate * (1.0 - 2.0 * sg))
            hidden_back[r, :] = (fb * lift * slope + tb * activated).astype(BF16)
            gate_back[r, :] = ((gdb * lift + tb * hidden) * slope + fb * hidden * lift * curve).astype(BF16)
            lift_back[r, :] = (fb * hidden * slope + gdb * activated).astype(BF16)

        by_chunk(step)

    def update_inner(b, c, m):
        if m == 0:
            first_back[...] = nt(k[b], whole[c, 0])
        elif m == 1:
            gated_back[...] = nn(target[b], whole[c, 1])
        else:
            third_back[...] = nt(k[b], whole[c, 2])

    def value_result(b, c):
        total = nt(gated[b], whole[c, 1]) + nn(hidden_back[...], w[b, 1])
        step = jnp.broadcast_to(s[b], (128, TOK)).T
        return jnp.concatenate([total[:, j * 128:(j + 1) * 128] * step for j in range(DIM // 128)], axis=1)

    def key_result(b, c):
        return (nn(ga[b], whole[c, 0]) + nn(gb[b], whole[c, 2])
                + nt(gate_back[...], w[b, 0]) + nt(lift_back[...], w[b, 2]))

    order = (0, 2, 1)
    arrived(("k", 1), ("w", 1, 0), ("w", 1, 2))
    forward_inner(1)
    arrived("s", ("v", 1), ("w", 1, 1))
    forward_target(1)
    forward_rest(1)
    pl.semaphore_wait(barrier, 2 * (SIDE - 1))
    for m in order:
        snd[D_LATE, m] = update_term(1, m).astype(BF16)
        rs_start(D_LATE, m)
    for m in order:
        own_columns(1, m)
    arrived(("k", 0), ("w", 0, 0), ("w", 0, 2))
    forward_inner(0)
    arrived(("v", 0), ("w", 0, 1))
    forward_target(0)
    forward_rest(0)
    for m in order:
        rs_middle(D_LATE, m)
    for m in order:
        own_columns(0, m)
    for m in order:
        renormed = own_update(1, m, rs_end(D_LATE, m))
        ag_start(R_LATE, m, renormed.astype(BF16))
    arrived(("q", 0), ("g", 0))
    a_out[...] = nn(q[0], w[1, 0])
    b_out[...] = nn(q[0], w[1, 2])
    for m in order:
        ag_middle(R_LATE, m)
    back_out[...] = nt(g[0], w[1, 1])
    output_step()
    c_early[0] = tn(ga_out[...], q[0])
    c_early[1] = tn(g[0], gated_out[...])
    c_early[2] = tn(gb_out[...], q[0])
    for m in order:
        snd[D_EARLY, m] = update_term(0, m).astype(BF16)
    stores.append(store_out(0, 0, nt(ga_out[...], w[1, 0]) + nt(gb_out[...], w[1, 2])))
    arrived(("q", 1), ("g", 1))
    ag_end(R_LATE, 0)
    a_out[...] = nt(q[1], whole[R_LATE, 0])
    ag_end(R_LATE, 2)
    b_out[...] = nt(q[1], whole[R_LATE, 2])
    ag_end(R_LATE, 1)
    back_out[...] = nn(g[1], whole[R_LATE, 1])
    rs_start(D_EARLY, 0)
    output_step()
    snd[C_LATE, 0] = tn(ga_out[...], q[1]).astype(BF16)
    rs_start(C_LATE, 0)
    snd[C_LATE, 2] = tn(gb_out[...], q[1]).astype(BF16)
    rs_start(C_LATE, 2)
    snd[C_LATE, 1] = tn(g[1], gated_out[...]).astype(BF16)
    rs_start(C_LATE, 1)
    stores.append(store_out(0, 1, nn(ga_out[...], whole[R_LATE, 0]) + nn(gb_out[...], whole[R_LATE, 2])))
    for m in order:
        rs_middle(C_LATE, m)
    for m in order:
        move, direct = renorm_back(1, m, rs_end(C_LATE, m))
        own_add[m] = move + direct
        ag_start(M_LATE, m, move.astype(BF16))
    for m in order:
        ag_middle(M_LATE, m)
    rs_middle(D_EARLY, 0)
    for m in order:
        ag_end(M_LATE, m)
        update_inner(1, M_LATE, m)
    rs_start(D_EARLY, 2)
    rs_start(D_EARLY, 1)
    update_step(1)
    snd[C_EARLY, 0] = (c_early[0] + tn(gate_back[...], k[1])).astype(BF16)
    rs_start(C_EARLY, 0)
    snd[C_EARLY, 2] = (c_early[2] + tn(lift_back[...], k[1])).astype(BF16)
    rs_start(C_EARLY, 2)
    snd[C_EARLY, 1] = (c_early[1] + tn(target[1], hidden_back[...])).astype(BF16)
    rs_start(C_EARLY, 1)
    rs_middle(D_EARLY, 2)
    rs_middle(D_EARLY, 1)
    stores.append(store_out(1, 1, key_result(1, M_LATE)))
    stores.append(store_out(2, 1, value_result(1, M_LATE)))
    for m in order:
        rs_middle(C_EARLY, m)
    for m in order:
        own_update(0, m, rs_end(D_EARLY, m))
    for m in order:
        move, _ = renorm_back(0, m, rs_end(C_EARLY, m) + own_add[m])
        ag_start(M_EARLY, m, move.astype(BF16))
    for m in order:
        ag_middle(M_EARLY, m)
    for m in order:
        ag_end(M_EARLY, m)
        update_inner(0, M_EARLY, m)
    update_step(0)
    stores.append(store_out(1, 0, key_result(0, M_EARLY)))
    stores.append(store_out(2, 0, value_result(0, M_EARLY)))
    for copies in started.values():
        for copy in copies:
            copy.wait_send()
    for copy in stores:
        copy.wait()


def local(queries, key_rows, value_rows, step_sizes, out_grads, first_saved, second_saved, third_saved):
    vectors = [a.reshape(2, TOK, DIM) for a in (queries, key_rows, value_rows)]
    matrices = [a.reshape(2, DIM, DIM) for a in (first_saved, second_saved, third_saved)]
    anywhere = pl.BlockSpec(memory_space=pl.ANY)

    def vmem(*shape, dtype=F32):
        return pltpu.VMEM(shape, dtype)

    sem = pltpu.SemaphoreType.DMA
    result = pl.pallas_call(
        kernel,
        out_shape=[jax.ShapeDtypeStruct((2 * TOK * DIM // 128, 128), F32)] * 3,
        in_specs=[anywhere] * 8,
        out_specs=[anywhere] * 3,
        scratch_shapes=[
            vmem(2, TOK, DIM, dtype=BF16), vmem(2, TOK, DIM, dtype=BF16), vmem(2, TOK, DIM, dtype=BF16),
            vmem(2, 1, TOK), vmem(2, TOK, DIM, dtype=BF16), vmem(2, 3, DIM, DIM, dtype=BF16),
            *[vmem(2, TOK, DIM)] * 4,
            *[vmem(2, TOK, DIM, dtype=BF16)] * 4,
            *[vmem(TOK, DIM)] * 3,
            *[vmem(TOK, DIM, dtype=BF16)] * 3,
            *[vmem(TOK, DIM)] * 3,
            *[vmem(TOK, DIM, dtype=BF16)] * 3,
            vmem(3, DIM, DIM),
            vmem(2, 3, 2 * OWN, DIM), vmem(2, 3, 2 * OWN, DIM), vmem(3, 2 * OWN, DIM),
            vmem(2, 3, 2 * OWN, 128), vmem(2, 3, 2 * OWN, 128),
            vmem(4, 3, DIM, DIM, dtype=BF16),
            vmem(4, 3, 2, SIDE - 1, BAND, DIM, dtype=BF16),
            vmem(4, 3, 2, BAND, DIM, dtype=BF16),
            vmem(4, 3, 2, SIDE - 1, OWN, DIM, dtype=BF16),
            vmem(3, 3, DIM, DIM, dtype=BF16),
            vmem(3, 2 * TOK * DIM // 128, 128),
            sem((17,)), sem((3, 2)),
            *[sem((4, 3, 2, SIDE - 1))] * 4,
            *[sem((3, 3, 2, SIDE - 1))] * 4,
        ],
        compiler_params=pltpu.CompilerParams(
            collective_id=0, has_side_effects=True, vmem_limit_bytes=60 * 2**20
        ),
        cost_estimate=pl.CostEstimate(flops=7 * 10**9, bytes_accessed=9 * 10**6, transcendentals=10**6),
    )(*vectors, step_sizes.reshape(2, 1, TOK), out_grads.reshape(2, TOK, DIM), *matrices)
    return tuple(part.reshape(2, TOK, 1, DIM) for part in result)


def solution(mesh):
    vectors, steps, matrices = P(None, "tok", "head", None), P(None, "tok", "head"), P(None, "head", None, None)
    return jax.shard_map(
        local,
        mesh=mesh,
        in_specs=(vectors, vectors, vectors, steps, vectors, matrices, matrices, matrices),
        out_specs=(vectors, vectors, vectors),
        check_vma=False,
    )
```

time: 789 us -> 103 us (0.13)
  waiting for transfers between devices: 429 us -> 0 us
  blocking collectives: 212 us -> 0 us
  Pallas kernels: 0 us -> 94.5 us
  matrix products: 48.8 us -> 0 us
  local copies, waits for them, and re-layouts: 53.8 us -> 5.58 us
  other arithmetic: 26.7 us -> 0 us
  between operations: 15.7 us -> 0.65 us
    unnamed x8 -> x0, waiting for transfers between devices: 201 us -> none
    all_gather x6 -> x0, blocking collectives: 138 us -> none  [rows_whole(): lax.all_gather(as_sent(values), 'tok', axis=1, tiled=True)]
    reduce_scatter x3 -> x0, waiting for transfers between devices: 119 us -> none  [cotangent_rows(): lax.psum_scatter(values[1].astype(jnp.bfloat16), 'tok', scatter_dimension...]
    psum x1 -> x0, waiting for transfers between devices: 109 us -> none  [restate(): lax.psum(pieces[0].astype(jnp.bfloat16), 'tok').astype(jnp.float32)]
    pallas_call x0 -> x1, Pallas kernels: none -> 94.5 us  [local(): pl.pallas_call(kernel, out_shape=[jax.ShapeDtypeStruct((2 * TOK * DIM //...]
    psum x2 -> x0, blocking collectives: 74 us -> none  [column_total(): return lax.psum(values, 'tok')]
    dot_general x49 -> x0, matrix products: 48.8 us -> none  [product(): jnp.einsum(pattern, left_side, right_side, preferred_element_type=jnp.flo...]
    unnamed x204 -> x7, local copies, waits for them, and re-layouts: 32.4 us -> 5.58 us
  transfers between devices with their start and end apart: 6 -> 0, of which waited for: 5 -> 0; matrix products, arithmetic and copies ran while one was open for 7% -> 0% of each run, Pallas kernels for 0% -> 0%
where the time goes in v1:
time: 103 us; the launch traced here: 101 us
  Pallas kernels  94.5 us (92%)
  local copies, waits for them, and re-layouts  5.58 us (5%)
    pallas_call x1, Pallas kernels, local(): pl.pallas_call(kernel, out_shape=[jax.ShapeDtypeStruct((2 * TOK * DIM //...  94.5 us
    unnamed x7, local copies, waits for them, and re-layouts  5.58 us

profile of v1, /device:TPU:2, one launch (start us, length us, event | category | flops | bytes accessed | tf_op | source)
XLA Modules:
  0.0 100.8 jit_solution(9647650194785835754)
XLA Ops:
  0.6 94.5 %shard_map.103 = (f32[2048,128]{1,0:T(8,128)}, f32[2048,128]{1,0:T(8,128)}, f32[2048,128]{1,0:T(8,128)}) custom-call(bf16[2,256,512]{2,1,0:T(8,128)(2,1)} %bitcast.17, bf16[2,256,512]{2,1,0:T(8,128)(2,1)} %bitcast.18, bf16[2,256,512]{2,1,0:T(8,128)(2,1)} %bitcast.19, f32[2,1,256]{2,1,0:T(1,128)} %bitcast.21, bf16[2,256,512]{2,1,0:T(8,128)(2,1)} %bitcast.20, ...), custom_call_target="tpu_custom_call" | custom-call | flops 7000000000 | bytes 9000000 | tf_op jit(solution)/shard_map/pallas_call | solution.py:369
  95.2 0.0 copy-start.1
  95.2 3.0 %copy.17 = f32[2,256,1,512]{3,2,1,0:T(1,128)} copy(f32[2,256,1,512]{3,2,1,0:T(1,128)} %bitcast.13) | data formatting | bytes 2097152
  98.2 0.0 copy-done.1
  98.2 0.0 copy-start
  98.2 1.0 copy.18
  99.2 0.6 copy-done
  99.8 1.0 copy.19
Async XLA Ops:
  95.2 3.0 %copy-start.1 = (f32[2048,128]{1,0:T(8,128)S(1)}, f32[2048,128]{1,0:T(8,128)}, u32[]{:S(2)}) copy-start(f32[2048,128]{1,0:T(8,128)} %get-tuple-element.7) | copy-start | bytes 3145732
  98.2 1.6 %copy-start = (f32[2048,128]{1,0:T(8,128)S(1)}, f32[2048,128]{1,0:T(8,128)}, u32[]{:S(2)}) copy-start(f32[2048,128]{1,0:T(8,128)} %get-tuple-element.8) | copy-start | bytes 3145732

commit v2 on v1

v2 whole, which is shorter than its diff:
```python
import functools

import jax
import jax.numpy as jnp
from jax import lax
from jax.experimental import pallas as pl
from jax.experimental.pallas import tpu as pltpu
from jax.sharding import PartitionSpec as P

EPSILON = 1e-06
MESH = pl.DeviceIdType.MESH
F32, BF16 = jnp.float32, jnp.bfloat16
SIDE = 4
TOK, DIM = 256, 512
HALF = DIM // 2
BAND = HALF // SIDE
OWN = BAND // SIDE
PARTS = 4
CHUNK = 16
D_LATE, C_LATE, C_EARLY, D_EARLY = range(4)
R_LATE, M_LATE, M_EARLY = range(3)


def nn(left, right):
    return lax.dot_general(left, right, (((1,), (0,)), ((), ())), preferred_element_type=F32)


def nt(left, right):
    return lax.dot_general(left, right, (((1,), (1,)), ((), ())), preferred_element_type=F32)


def tn(left, right):
    return lax.dot_general(left, right, (((0,), (0,)), ((), ())), preferred_element_type=F32)


def kernel(
    q_any, k_any, v_any, s_any, g_any, w1_any, w2_any, w3_any,
    query_any, key_any, value_any,
    q, k, v, s, g, w,
    a_in, b_in, back, factors, gated, target, ga, gb,
    a_out, b_out, back_out, gated_out, ga_out, gb_out,
    first_back, third_back, gated_back, gate_back, hidden_back, lift_back,
    c_early, own_w, own_p, own_add, kept, summed,
    snd, passing, passed, got1, mid, got2, whole, out,
    in_sem, out_sem, send_sem, recv_sem,
):
    tok = lax.axis_index("tok")
    x, y = lax.rem(tok, SIDE), tok // SIDE
    along_x = [(y * SIDE + lax.rem(x + d, SIDE), lax.rem(x + d, SIDE)) for d in range(1, SIDE)]
    along_y = [(lax.rem(y + d, SIDE) * SIDE + x, lax.rem(y + d, SIDE)) for d in range(1, SIDE)]

    weights_any = (w1_any, w2_any, w3_any)
    loads = {}

    def load(name, source, place):
        copy = pltpu.make_async_copy(source, place, in_sem.at[len(loads)])
        copy.start()
        loads[name] = copy

    def arrived(*names):
        for name in names:
            loads[name].wait()

    load("s", s_any, s)
    for b in (1, 0):
        load(("k", b), k_any.at[b], k.at[b])
        load(("w", b, 0), weights_any[0].at[b], w.at[b, 0])
        load(("w", b, 2), weights_any[2].at[b], w.at[b, 2])
        load(("v", b), v_any.at[b], v.at[b])
        load(("w", b, 1), weights_any[1].at[b], w.at[b, 1])
    for b in (0, 1):
        load(("q", b), q_any.at[b], q.at[b])
        load(("g", b), g_any.at[b], g.at[b])

    barrier = pltpu.get_barrier_semaphore()
    for peer, _ in along_x + along_y:
        pl.semaphore_signal(barrier, inc=1, device_id={"tok": peer}, device_id_type=MESH)

    started = {}
    sem_count = [0]

    def send(name, source, place, peer):
        n = sem_count[0]
        sem_count[0] = n + 1
        copy = pltpu.make_async_remote_copy(
            src_ref=source, dst_ref=place, send_sem=send_sem.at[n], recv_sem=recv_sem.at[n],
            device_id={"tok": peer}, device_id_type=MESH,
        )
        copy.start()
        started.setdefault(name, []).append(copy)

    def received(name):
        for copy in started[name]:
            copy.wait_recv()

    def rows(start, size):
        return pl.ds(pl.multiple_of(start, OWN), size)

    def ring(peers):
        return peers[0], peers[1], peers[2]

    firsts = ((0, x, along_x, along_y), (1, y, along_y, along_x))
    UPPER, LOWER = 0, BAND // 2

    def rs_start(c, m):
        for half, _, peers, _ in firsts:
            (right, at_right), (_, at_far), (left, at_left) = ring(peers)
            far, near_right, near_left = (half * HALF + at * BAND for at in (at_far, at_right, at_left))
            send(("far", c, m, half, 0), snd.at[c, m, rows(far + UPPER, BAND // 2)], passing.at[c, m, half, 0], right)
            send(("far", c, m, half, 1), snd.at[c, m, rows(far + LOWER, BAND // 2)], passing.at[c, m, half, 1], left)
            send(("near", c, m, half), snd.at[c, m, rows(near_right + LOWER, BAND // 2)],
                 got1.at[c, m, half, 0, pl.ds(LOWER, BAND // 2)], right)
            send(("near", c, m, half), snd.at[c, m, rows(near_left + UPPER, BAND // 2)],
                 got1.at[c, m, half, 1, pl.ds(UPPER, BAND // 2)], left)

    def rs_relay(c, m):
        for half, _, peers, _ in firsts:
            (right, at_right), _, (left, at_left) = ring(peers)
            for side, peer, at, part in ((0, right, at_right, UPPER), (1, left, at_left, LOWER)):
                received(("far", c, m, half, side))
                mine = snd[c, m, rows(half * HALF + at * BAND + part, BAND // 2), :].astype(F32)
                passed[c, m, half, side] = (mine + passing[c, m, half, side].astype(F32)).astype(BF16)
                send(("near", c, m, half), passed.at[c, m, half, side],
                     got1.at[c, m, half, side, pl.ds(part, BAND // 2)], peer)

    def rs_middle(c, m):
        for half, mine, _, peers in firsts:
            received(("near", c, m, half))
            total = (snd[c, m, rows(half * HALF + mine * BAND, BAND), :].astype(F32)
                     + got1[c, m, half, 0].astype(F32) + got1[c, m, half, 1].astype(F32))
            mid[c, m, half] = total.astype(BF16)
            for d, (peer, at) in enumerate(peers):
                send(("rs2", c, m, half), mid.at[c, m, half, rows(at * OWN, OWN)], got2.at[c, m, half, d], peer)

    def rs_end(c, m):
        parts = []
        for half, mine in ((0, y), (1, x)):
            received(("rs2", c, m, half))
            total = mid[c, m, half, rows(mine * OWN, OWN), :].astype(F32)
            for d in range(SIDE - 1):
                total = total + got2[c, m, half, d].astype(F32)
            parts.append(total)
        return jnp.concatenate(parts, axis=0)

    own_rows = (x * BAND + y * OWN, HALF + y * BAND + x * OWN)

    def ag_start(c, m, value):
        for half, _, _, peers in firsts:
            whole[c, m, rows(own_rows[half], OWN), :] = value[half * OWN:(half + 1) * OWN]
            for peer, _ in peers:
                place = whole.at[c, m, rows(own_rows[half], OWN)]
                send(("ag1", c, m, half), place, place, peer)

    def ag_middle(c, m):
        for half, mine, peers, _ in firsts:
            received(("ag1", c, m, half))
            (right, _), _, (left, _) = ring(peers)
            for peer, side, part in ((right, 0, UPPER), (left, 1, LOWER), (right, 0, LOWER), (left, 1, UPPER)):
                place = whole.at[c, m, rows(half * HALF + mine * BAND + part, BAND // 2)]
                early = (side, part) in ((0, UPPER), (1, LOWER))
                send(("ag2", c, m, half, side) if early else ("ag3", c, m, half), place, place, peer)

    def ag_relay(c, m):
        for half, _, peers, _ in firsts:
            (right, at_right), _, (left, at_left) = ring(peers)
            for side, peer, at, part in ((0, right, at_left, UPPER), (1, left, at_right, LOWER)):
                received(("ag2", c, m, half, side))
                place = whole.at[c, m, rows(half * HALF + at * BAND + part, BAND // 2)]
                send(("ag3", c, m, half), place, place, peer)

    def ag_end(c, m):
        for half in (0, 1):
            received(("ag3", c, m, half))

    def by_chunk(step):
        def body(i, carry):
            step(rows(i * CHUNK, CHUNK))
            return carry

        lax.fori_loop(0, TOK // CHUNK, body, 0)

    def forward_inner(b):
        a_in[b] = nn(k[b], w[b, 0])
        b_in[b] = nn(k[b], w[b, 2])

    def forward_target(b):
        step = jnp.broadcast_to(s[b], (128, TOK)).T
        for j in range(DIM // 128):
            lanes = slice(j * 128, (j + 1) * 128)
            target[b, :, lanes] = (step * v[b, :, lanes].astype(F32)).astype(BF16)

    def gate_step(gate, lift):
        sg = jax.nn.sigmoid(gate)
        activated = gate * sg
        return activated, lift * (sg * (1.0 + gate * (1.0 - sg)))

    def forward_rest(b):
        back[b] = nt(target[b], w[b, 1])

        def step(r):
            lift, hidden = b_in[b, r, :], back[b, r, :]
            activated, sloped = gate_step(a_in[b, r, :], lift)
            gated[b, r, :] = (activated * lift).astype(BF16)
            ga[b, r, :] = (hidden * sloped).astype(BF16)
            gb[b, r, :] = (hidden * activated).astype(BF16)

        by_chunk(step)

    def update_factors(b):
        def step(r):
            gate, lift, hidden = a_in[b, r, :], b_in[b, r, :], back[b, r, :]
            sg = jax.nn.sigmoid(gate)
            rest = 1.0 - sg
            slope = sg * (1.0 + gate * rest)
            curve = sg * rest * (2.0 + gate * (1.0 - 2.0 * sg))
            factors[0, r, :] = gate * sg
            factors[1, r, :] = lift * slope
            factors[2, r, :] = hidden * slope
            factors[3, r, :] = hidden * lift * curve

        by_chunk(step)

    def update_term(b, m):
        if m == 0:
            return tn(ga[b], k[b])
        if m == 1:
            return tn(target[b], gated[b])
        return tn(gb[b], k[b])

    row_of = lax.broadcasted_iota(jnp.int32, (2 * OWN, DIM), 0)
    col_of = lax.broadcasted_iota(jnp.int32, (2 * OWN, DIM), 1)
    wanted = jnp.where(row_of < OWN, own_rows[0] + row_of, own_rows[1] + row_of - OWN)
    picker = jnp.where(col_of == wanted, 1.0, 0.0).astype(BF16)

    def own_columns(b, m):
        mine = nt(picker, w[b, m])
        own_w[b, m] = mine
        kept[b, m] = jnp.broadcast_to(jnp.sqrt(jnp.sum(mine * mine, axis=1, keepdims=True) + EPSILON), (2 * OWN, 128))

    def own_update(b, m, change):
        total = own_w[b, m] + change
        own_p[b, m] = total
        summed[b, m] = jnp.broadcast_to(jnp.sqrt(jnp.sum(total * total, axis=1, keepdims=True) + EPSILON), (2 * OWN, 128))
        return total * (kept[b, m, :, :1] / summed[b, m, :, :1])

    def renorm_back(b, m, cotangent):
        matrix, before, after = own_p[b, m], kept[b, m, :, :1], summed[b, m, :, :1]
        inner = jnp.sum(cotangent * matrix, axis=1, keepdims=True)
        factor = before / after
        move = cotangent * factor - matrix * (factor * inner / (after * after))
        return move, own_w[b, m] * (inner / (after * before))

    def output_first():
        def step(r):
            lift = b_out[r, :]
            activated, sloped = gate_step(a_out[r, :], lift)
            gated_out[r, :] = (activated * lift).astype(BF16)
            a_out[r, :] = activated
            b_out[r, :] = sloped

        by_chunk(step)

    def output_second():
        def step(r):
            hidden = back_out[r, :]
            ga_out[r, :] = (hidden * b_out[r, :]).astype(BF16)
            gb_out[r, :] = (hidden * a_out[r, :]).astype(BF16)

        by_chunk(step)

    def store_out(i, b, value):
        for j in range(DIM // 128):
            out[i, pl.ds(b * TOK * 4 + j, TOK, stride=4), :] = value[:, j * 128:(j + 1) * 128]
        place = pl.ds(b * TOK * 4, TOK * 4)
        target_any = (query_any, key_any, value_any)[i]
        copy = pltpu.make_async_copy(out.at[i, place], target_any.at[place], out_sem.at[i, b])
        copy.start()
        return copy

    stores = []

    def hidden_step():
        def step(r):
            hidden_back[r, :] = (first_back[r, :] * factors[1, r, :] + third_back[r, :] * factors[0, r, :]).astype(BF16)

        by_chunk(step)

    def lift_step():
        def step(r):
            lift_back[r, :] = (first_back[r, :] * factors[2, r, :] + gated_back[r, :] * factors[0, r, :]).astype(BF16)

        by_chunk(step)

    def gate_backward():
        def step(r):
            gate_back[r, :] = (gated_back[r, :] * factors[1, r, :] + third_back[r, :] * factors[2, r, :]
                               + first_back[r, :] * factors[3, r, :]).astype(BF16)

        by_chunk(step)

    def update_inner(b, c, m):
        if m == 0:
            first_back[...] = nt(k[b], whole[c, 0])
        elif m == 1:
            gated_back[...] = nn(target[b], whole[c, 1])
        else:
            third_back[...] = nt(k[b], whole[c, 2])

    def scaled(b, total):
        step = jnp.broadcast_to(s[b], (128, TOK)).T
        return jnp.concatenate([total[:, j * 128:(j + 1) * 128] * step for j in range(DIM // 128)], axis=1)

    def start_term(m):
        if m == 0:
            return tn(gate_back[...], k[1])
        if m == 1:
            return tn(target[1], hidden_back[...])
        return tn(lift_back[...], k[1])

    def each(action, c, order):
        for m in order:
            action(c, m)

    order = (0, 2, 1)
    arrived(("k", 1), ("w", 1, 0), ("w", 1, 2))
    forward_inner(1)
    arrived("s", ("v", 1), ("w", 1, 1))
    forward_target(1)
    forward_rest(1)
    pl.semaphore_wait(barrier, 2 * (SIDE - 1))
    for m in (0, 2, 1):
        snd[D_LATE, m] = update_term(1, m).astype(BF16)
        rs_start(D_LATE, m)
    for m in (0, 2, 1):
        own_columns(1, m)
    arrived(("k", 0), ("w", 0, 0), ("w", 0, 2))
    forward_inner(0)
    rs_relay(D_LATE, 0)
    arrived(("v", 0), ("w", 0, 1))
    forward_target(0)
    rs_relay(D_LATE, 2)
    forward_rest(0)
    rs_relay(D_LATE, 1)
    each(rs_middle, D_LATE, (0, 2, 1))
    snd[D_EARLY, 0] = update_term(0, 0).astype(BF16)
    rs_start(D_EARLY, 0)
    snd[D_EARLY, 2] = update_term(0, 2).astype(BF16)
    for m in (0, 2, 1):
        renormed = own_update(1, m, rs_end(D_LATE, m))
        ag_start(R_LATE, m, renormed.astype(BF16))
    rs_start(D_EARLY, 2)
    snd[D_EARLY, 1] = update_term(0, 1).astype(BF16)
    arrived(("q", 0), ("g", 0))
    a_out[...] = nn(q[0], w[1, 0])
    b_out[...] = nn(q[0], w[1, 2])
    each(ag_middle, R_LATE, (0, 2, 1))
    back_out[...] = nt(g[0], w[1, 1])
    output_first()
    ag_relay(R_LATE, 0)
    output_second()
    ag_relay(R_LATE, 2)
    c_early[0] = tn(ga_out[...], q[0])
    ag_relay(R_LATE, 1)
    c_early[1] = tn(g[0], gated_out[...])
    c_early[2] = tn(gb_out[...], q[0])
    stores.append(store_out(0, 0, nt(ga_out[...], w[1, 0]) + nt(gb_out[...], w[1, 2])))
    for m in (0, 2, 1):
        own_columns(0, m)
    arrived(("q", 1), ("g", 1))
    ag_end(R_LATE, 0)
    a_out[...] = nt(q[1], whole[R_LATE, 0])
    ag_end(R_LATE, 2)
    b_out[...] = nt(q[1], whole[R_LATE, 2])
    output_first()
    snd[C_LATE, 1] = tn(g[1], gated_out[...]).astype(BF16)
    rs_start(C_LATE, 1)
    ag_end(R_LATE, 1)
    back_out[...] = nn(g[1], whole[R_LATE, 1])
    output_second()
    snd[C_LATE, 0] = tn(ga_out[...], q[1]).astype(BF16)
    rs_start(C_LATE, 0)
    snd[C_LATE, 2] = tn(gb_out[...], q[1]).astype(BF16)
    rs_start(C_LATE, 2)
    each(rs_relay, C_LATE, (1, 0, 2))
    rs_start(D_EARLY, 1)
    rs_relay(D_EARLY, 0)
    rs_relay(D_EARLY, 2)
    each(rs_middle, C_LATE, (1, 0, 2))
    stores.append(store_out(0, 1, nn(ga_out[...], whole[R_LATE, 0]) + nn(gb_out[...], whole[R_LATE, 2])))
    for m in (1, 0, 2):
        move, direct = renorm_back(1, m, rs_end(C_LATE, m))
        own_add[m] = move + direct
        ag_start(M_LATE, m, move.astype(BF16))
    update_factors(1)
    each(ag_middle, M_LATE, (1, 0, 2))
    rs_middle(D_EARLY, 0)
    rs_middle(D_EARLY, 2)
    rs_relay(D_EARLY, 1)
    each(ag_relay, M_LATE, (1, 0, 2))
    ag_end(M_LATE, 1)
    gated_back[...] = nn(target[1], whole[M_LATE, 1])
    ag_end(M_LATE, 0)
    first_back[...] = nt(k[1], whole[M_LATE, 0])
    lift_step()
    snd[C_EARLY, 2] = (c_early[2] + start_term(2)).astype(BF16)
    rs_start(C_EARLY, 2)
    ag_end(M_LATE, 2)
    third_back[...] = nt(k[1], whole[M_LATE, 2])
    gate_backward()
    snd[C_EARLY, 0] = (c_early[0] + start_term(0)).astype(BF16)
    rs_start(C_EARLY, 0)
    hidden_step()
    snd[C_EARLY, 1] = (c_early[1] + start_term(1)).astype(BF16)
    rs_start(C_EARLY, 1)
    each(rs_relay, C_EARLY, (2, 0, 1))
    rs_middle(D_EARLY, 1)
    each(rs_middle, C_EARLY, (2, 0, 1))
    stores.append(store_out(1, 1, nn(ga[1], whole[M_LATE, 0]) + nn(gb[1], whole[M_LATE, 2])
                            + nt(gate_back[...], w[1, 0]) + nt(lift_back[...], w[1, 2])))
    for m in (0, 2, 1):
        own_update(0, m, rs_end(D_EARLY, m))
    for m in (2, 0, 1):
        move, _ = renorm_back(0, m, rs_end(C_EARLY, m) + own_add[m])
        ag_start(M_EARLY, m, move.astype(BF16))
    stores.append(store_out(2, 1, scaled(1, nt(gated[1], whole[M_LATE, 1]) + nn(hidden_back[...], w[1, 1]))))
    each(ag_middle, M_EARLY, (2, 0, 1))
    update_factors(0)
    each(ag_relay, M_EARLY, (2, 0, 1))
    ag_end(M_EARLY, 2)
    third_back[...] = nt(k[0], whole[M_EARLY, 2])
    ag_end(M_EARLY, 0)
    first_back[...] = nt(k[0], whole[M_EARLY, 0])
    hidden_step()
    key_part = nn(ga[0], whole[M_EARLY, 0]) + nn(gb[0], whole[M_EARLY, 2])
    value_part = nn(hidden_back[...], w[0, 1])
    ag_end(M_EARLY, 1)
    gated_back[...] = nn(target[0], whole[M_EARLY, 1])
    lift_step()
    gate_backward()
    stores.append(store_out(1, 0, key_part + nt(gate_back[...], w[0, 0]) + nt(lift_back[...], w[0, 2])))
    stores.append(store_out(2, 0, scaled(0, value_part + nt(gated[0], whole[M_EARLY, 1]))))
    for copies in started.values():
        for copy in copies:
            copy.wait_send()
    for copy in stores:
        copy.wait()


def hand_out(query_any, key_any, value_any, query_out, key_out, value_out, held, in_sem, out_sem):
    size = held.shape[1] // PARTS
    pairs = ((query_any, query_out), (key_any, key_out), (value_any, value_out))
    loads, stores = [], []
    for i, (source, place) in enumerate(pairs):
        for j in range(PARTS):
            part = pl.ds(j * size, size)
            loads.append(pltpu.make_async_copy(source.at[part], held.at[i, part], in_sem.at[i, j]))
            stores.append(pltpu.make_async_copy(held.at[i, part], place.at[part], out_sem.at[i, j]))
    for copy in loads:
        copy.start()
    for load, store in zip(loads, stores):
        load.wait()
        store.start()
    for copy in stores:
        copy.wait()


def local(queries, key_rows, value_rows, step_sizes, out_grads, first_saved, second_saved, third_saved):
    vectors = [a.reshape(2, TOK, DIM) for a in (queries, key_rows, value_rows)]
    matrices = [a.reshape(2, DIM, DIM) for a in (first_saved, second_saved, third_saved)]
    anywhere = pl.BlockSpec(memory_space=pl.ANY)

    def vmem(*shape, dtype=F32):
        return pltpu.VMEM(shape, dtype)

    sem = pltpu.SemaphoreType.DMA
    result = pl.pallas_call(
        kernel,
        out_shape=[jax.ShapeDtypeStruct((2 * TOK * DIM // 128, 128), F32)] * 3,
        in_specs=[anywhere] * 8,
        out_specs=[anywhere] * 3,
        scratch_shapes=[
            vmem(2, TOK, DIM, dtype=BF16), vmem(2, TOK, DIM, dtype=BF16), vmem(2, TOK, DIM, dtype=BF16),
            vmem(2, 1, TOK), vmem(2, TOK, DIM, dtype=BF16), vmem(2, 3, DIM, DIM, dtype=BF16),
            *[vmem(2, TOK, DIM)] * 3, vmem(4, TOK, DIM),
            *[vmem(2, TOK, DIM, dtype=BF16)] * 4,
            *[vmem(TOK, DIM)] * 3,
            *[vmem(TOK, DIM, dtype=BF16)] * 3,
            *[vmem(TOK, DIM)] * 3,
            *[vmem(TOK, DIM, dtype=BF16)] * 3,
            vmem(3, DIM, DIM),
            vmem(2, 3, 2 * OWN, DIM), vmem(2, 3, 2 * OWN, DIM), vmem(3, 2 * OWN, DIM),
            vmem(2, 3, 2 * OWN, 128), vmem(2, 3, 2 * OWN, 128),
            vmem(4, 3, DIM, DIM, dtype=BF16),
            vmem(4, 3, 2, 2, BAND // 2, DIM, dtype=BF16),
            vmem(4, 3, 2, 2, BAND // 2, DIM, dtype=BF16),
            vmem(4, 3, 2, 2, BAND, DIM, dtype=BF16),
            vmem(4, 3, 2, BAND, DIM, dtype=BF16),
            vmem(4, 3, 2, SIDE - 1, OWN, DIM, dtype=BF16),
            vmem(3, 3, DIM, DIM, dtype=BF16),
            vmem(3, 2 * TOK * DIM // 128, 128),
            sem((17,)), sem((3, 2)), sem((378,)), sem((378,)),
        ],
        compiler_params=pltpu.CompilerParams(
            collective_id=0, has_side_effects=True, vmem_limit_bytes=60 * 2**20
        ),
        cost_estimate=pl.CostEstimate(flops=7 * 10**9, bytes_accessed=9 * 10**6, transcendentals=10**6),
    )(*vectors, step_sizes.reshape(2, 1, TOK), out_grads.reshape(2, TOK, DIM), *matrices)
    result = pl.pallas_call(
        hand_out,
        out_shape=[jax.ShapeDtypeStruct((2 * TOK * DIM // 128, 128), F32)] * 3,
        in_specs=[anywhere] * 3,
        out_specs=[anywhere] * 3,
        scratch_shapes=[vmem(3, 2 * TOK * DIM // 128, 128), sem((3, PARTS)), sem((3, PARTS))],
        cost_estimate=pl.CostEstimate(flops=0, bytes_accessed=6 * 10**6, transcendentals=0),
    )(*result)
    return tuple(part.reshape(2, TOK, 1, DIM) for part in result)


def solution(mesh):
    vectors, steps, matrices = P(None, "tok", "head", None), P(None, "tok", "head"), P(None, "head", None, None)
    return jax.shard_map(
        local,
        mesh=mesh,
        in_specs=(vectors, vectors, vectors, steps, vectors, matrices, matrices, matrices),
        out_specs=(vectors, vectors, vectors),
        check_vma=False,
    )
```

time: 103 us -> 96.8 us (0.940)
  local copies, waits for them, and re-layouts: 5.58 us -> 0 us
    unnamed x7 -> x0, local copies, waits for them, and re-layouts: 5.58 us -> none
    pallas_call x1, Pallas kernels: 94.5 us -> 91.7 us  [local(): pl.pallas_call(kernel, out_shape=[jax.ShapeDtypeStruct((2 * TOK * DIM //...]
    pallas_call x0 -> x1, Pallas kernels: none -> 2.81 us  [local(): pl.pallas_call(hand_out, out_shape=[jax.ShapeDtypeStruct((2 * TOK * DIM /...]
where the time goes in v2:
time: 96.8 us; the launch traced here: 95.3 us
  Pallas kernels  94.5 us (98%)
    pallas_call x1, Pallas kernels, local(): pl.pallas_call(kernel, out_shape=[jax.ShapeDtypeStruct((2 * TOK * DIM //...  91.7 us
    pallas_call x1, Pallas kernels, local(): pl.pallas_call(hand_out, out_shape=[jax.ShapeDtypeStruct((2 * TOK * DIM /...  2.81 us

profile of v2, /device:TPU:2, one launch (start us, length us, event | category | flops | bytes accessed | tf_op | source)
XLA Modules:
  0.0 95.3 jit_solution(9376284582363871308)
XLA Ops:
  0.6 91.7 %shard_map.103 = (f32[2048,128]{1,0:T(8,128)}, f32[2048,128]{1,0:T(8,128)}, f32[2048,128]{1,0:T(8,128)}) custom-call(bf16[2,256,512]{2,1,0:T(8,128)(2,1)} %bitcast.17, bf16[2,256,512]{2,1,0:T(8,128)(2,1)} %bitcast.18, bf16[2,256,512]{2,1,0:T(8,128)(2,1)} %bitcast.19, f32[2,1,256]{2,1,0:T(1,128)} %bitcast.21, bf16[2,256,512]{2,1,0:T(8,128)(2,1)} %bitcast.20, ...), custom_call_target="tpu_custom_call" | custom-call | flops 7000000000 | bytes 9000000 | tf_op jit(solution)/shard_map/pallas_call | solution.py:476
  92.3 2.8 %shard_map.104 = (f32[2048,128]{1,0:T(8,128)}, f32[2048,128]{1,0:T(8,128)}, f32[2048,128]{1,0:T(8,128)}) custom-call(f32[2048,128]{1,0:T(8,128)} %get-tuple-element.9.query_any, f32[2048,128]{1,0:T(8,128)} %get-tuple-element.10.key_any, f32[2048,128]{1,0:T(8,128)} %get-tuple-element.11.value_any), custom_call_target="tpu_custom_call" | custom-call | bytes 6000000 | tf_op jit(solution)/shard_map/pallas_call | solution.py:508

commit v3 on v2

--- a/solution.py
+++ b/solution.py
@@ -35,14 +35,14 @@
 
 def kernel(
     q_any, k_any, v_any, s_any, g_any, w1_any, w2_any, w3_any,
-    query_any, key_any, value_any,
+    query_out, key_out, value_out,
     q, k, v, s, g, w,
     a_in, b_in, back, factors, gated, target, ga, gb,
-    a_out, b_out, back_out, gated_out, ga_out, gb_out,
+    a_out, b_out, back_out, gated_out, ga_out, gb_out, ga_early, gb_early,
     first_back, third_back, gated_back, gate_back, hidden_back, lift_back,
     c_early, own_w, own_p, own_add, kept, summed,
-    snd, passing, passed, got1, mid, got2, whole, out,
-    in_sem, out_sem, send_sem, recv_sem,
+    snd, passing, passed, got1, mid, got2, whole,
+    in_sem, send_sem, recv_sem,
 ):
     tok = lax.axis_index("tok")
     x, y = lax.rem(tok, SIDE), tok // SIDE
@@ -177,7 +177,7 @@
             step(rows(i * CHUNK, CHUNK))
             return carry
 
-        lax.fori_loop(0, TOK // CHUNK, body, 0)
+        lax.fori_loop(0, TOK // CHUNK, body, 0, unroll=2)
 
     def forward_inner(b):
         a_in[b] = nn(k[b], w[b, 0])
@@ -260,24 +260,18 @@
 
         by_chunk(step)
 
-    def output_second():
+    def output_second(ga_place, gb_place):
         def step(r):
             hidden = back_out[r, :]
-            ga_out[r, :] = (hidden * b_out[r, :]).astype(BF16)
-            gb_out[r, :] = (hidden * a_out[r, :]).astype(BF16)
+            ga_place[r, :] = (hidden * b_out[r, :]).astype(BF16)
+            gb_place[r, :] = (hidden * a_out[r, :]).astype(BF16)
 
         by_chunk(step)
 
     def store_out(i, b, value):
+        place = (query_out, key_out, value_out)[i]
         for j in range(DIM // 128):
-            out[i, pl.ds(b * TOK * 4 + j, TOK, stride=4), :] = value[:, j * 128:(j + 1) * 128]
-        place = pl.ds(b * TOK * 4, TOK * 4)
-        target_any = (query_any, key_any, value_any)[i]
-        copy = pltpu.make_async_copy(out.at[i, place], target_any.at[place], out_sem.at[i, b])
-        copy.start()
-        return copy
-
-    stores = []
+            place[pl.ds(b * TOK * 4 + j, TOK, stride=4), :] = value[:, j * 128:(j + 1) * 128]
 
     def hidden_step():
         def step(r):
@@ -357,15 +351,15 @@
     back_out[...] = nt(g[0], w[1, 1])
     output_first()
     ag_relay(R_LATE, 0)
-    output_second()
+    output_second(ga_early, gb_early)
     ag_relay(R_LATE, 2)
-    c_early[0] = tn(ga_out[...], q[0])
+    c_early[0] = tn(ga_early[...], q[0])
+    c_early[2] = tn(gb_early[...], q[0])
     ag_relay(R_LATE, 1)
+    rs_start(D_EARLY, 1)
+    rs_relay(D_EARLY, 0)
+    rs_relay(D_EARLY, 2)
     c_early[1] = tn(g[0], gated_out[...])
-    c_early[2] = tn(gb_out[...], q[0])
-    stores.append(store_out(0, 0, nt(ga_out[...], w[1, 0]) + nt(gb_out[...], w[1, 2])))
-    for m in (0, 2, 1):
-        own_columns(0, m)
     arrived(("q", 1), ("g", 1))
     ag_end(R_LATE, 0)
     a_out[...] = nt(q[1], whole[R_LATE, 0])
@@ -376,27 +370,31 @@
     rs_start(C_LATE, 1)
     ag_end(R_LATE, 1)
     back_out[...] = nn(g[1], whole[R_LATE, 1])
-    output_second()
+    output_second(ga_out, gb_out)
     snd[C_LATE, 0] = tn(ga_out[...], q[1]).astype(BF16)
     rs_start(C_LATE, 0)
     snd[C_LATE, 2] = tn(gb_out[...], q[1]).astype(BF16)
     rs_start(C_LATE, 2)
-    each(rs_relay, C_LATE, (1, 0, 2))
-    rs_start(D_EARLY, 1)
-    rs_relay(D_EARLY, 0)
-    rs_relay(D_EARLY, 2)
+    own_columns(0, 0)
+    rs_relay(C_LATE, 1)
+    own_columns(0, 2)
+    rs_relay(C_LATE, 0)
+    own_columns(0, 1)
+    rs_relay(C_LATE, 2)
     each(rs_middle, C_LATE, (1, 0, 2))
-    stores.append(store_out(0, 1, nn(ga_out[...], whole[R_LATE, 0]) + nn(gb_out[...], whole[R_LATE, 2])))
+    rs_relay(D_EARLY, 1)
+    store_out(0, 1, nn(ga_out[...], whole[R_LATE, 0]) + nn(gb_out[...], whole[R_LATE, 2]))
     for m in (1, 0, 2):
         move, direct = renorm_back(1, m, rs_end(C_LATE, m))
         own_add[m] = move + direct
         ag_start(M_LATE, m, move.astype(BF16))
+    rs_middle(D_EARLY, 0)
+    rs_middle(D_EARLY, 2)
     update_factors(1)
     each(ag_middle, M_LATE, (1, 0, 2))
-    rs_middle(D_EARLY, 0)
-    rs_middle(D_EARLY, 2)
-    rs_relay(D_EARLY, 1)
+    store_out(0, 0, nt(ga_early[...], w[1, 0]) + nt(gb_early[...], w[1, 2]))
     each(ag_relay, M_LATE, (1, 0, 2))
+    rs_middle(D_EARLY, 1)
     ag_end(M_LATE, 1)
     gated_back[...] = nn(target[1], whole[M_LATE, 1])
     ag_end(M_LATE, 0)
@@ -413,16 +411,15 @@
     snd[C_EARLY, 1] = (c_early[1] + start_term(1)).astype(BF16)
     rs_start(C_EARLY, 1)
     each(rs_relay, C_EARLY, (2, 0, 1))
-    rs_middle(D_EARLY, 1)
     each(rs_middle, C_EARLY, (2, 0, 1))
-    stores.append(store_out(1, 1, nn(ga[1], whole[M_LATE, 0]) + nn(gb[1], whole[M_LATE, 2])
-                            + nt(gate_back[...], w[1, 0]) + nt(lift_back[...], w[1, 2])))
+    store_out(1, 1, nn(ga[1], whole[M_LATE, 0]) + nn(gb[1], whole[M_LATE, 2])
+              + nt(gate_back[...], w[1, 0]) + nt(lift_back[...], w[1, 2]))
     for m in (0, 2, 1):
         own_update(0, m, rs_end(D_EARLY, m))
     for m in (2, 0, 1):
         move, _ = renorm_back(0, m, rs_end(C_EARLY, m) + own_add[m])
         ag_start(M_EARLY, m, move.astype(BF16))
-    stores.append(store_out(2, 1, scaled(1, nt(gated[1], whole[M_LATE, 1]) + nn(hidden_back[...], w[1, 1]))))
+    store_out(2, 1, scaled(1, nt(gated[1], whole[M_LATE, 1]) + nn(hidden_back[...], w[1, 1])))
     each(ag_middle, M_EARLY, (2, 0, 1))
     update_factors(0)
     each(ag_relay, M_EARLY, (2, 0, 1))
@@ -437,30 +434,23 @@
     gated_back[...] = nn(target[0], whole[M_EARLY, 1])
     lift_step()
     gate_backward()
-    stores.append(store_out(1, 0, key_part + nt(gate_back[...], w[0, 0]) + nt(lift_back[...], w[0, 2])))
-    stores.append(store_out(2, 0, scaled(0, value_part + nt(gated[0], whole[M_EARLY, 1]))))
+    store_out(1, 0, key_part + nt(gate_back[...], w[0, 0]) + nt(lift_back[...], w[0, 2]))
+    store_out(2, 0, scaled(0, value_part + nt(gated[0], whole[M_EARLY, 1])))
     for copies in started.values():
         for copy in copies:
             copy.wait_send()
-    for copy in stores:
-        copy.wait()
-
-
-def hand_out(query_any, key_any, value_any, query_out, key_out, value_out, held, in_sem, out_sem):
-    size = held.shape[1] // PARTS
-    pairs = ((query_any, query_out), (key_any, key_out), (value_any, value_out))
-    loads, stores = [], []
+
+
+def hand_out(query_ref, key_ref, value_ref, query_out, key_out, value_out, sems):
+    pairs = ((query_ref, query_out), (key_ref, key_out), (value_ref, value_out))
+    copies = []
     for i, (source, place) in enumerate(pairs):
         for j in range(PARTS):
-            part = pl.ds(j * size, size)
-            loads.append(pltpu.make_async_copy(source.at[part], held.at[i, part], in_sem.at[i, j]))
-            stores.append(pltpu.make_async_copy(held.at[i, part], place.at[part], out_sem.at[i, j]))
-    for copy in loads:
+            part = pl.ds(j * (source.shape[0] // PARTS), source.shape[0] // PARTS)
+            copies.append(pltpu.make_async_copy(source.at[part], place.at[part], sems.at[i, j]))
+    for copy in copies:
         copy.start()
-    for load, store in zip(loads, stores):
-        load.wait()
-        store.start()
-    for copy in stores:
+    for copy in copies:
         copy.wait()
 
 
@@ -475,16 +465,16 @@
     sem = pltpu.SemaphoreType.DMA
     result = pl.pallas_call(
         kernel,
-        out_shape=[jax.ShapeDtypeStruct((2 * TOK * DIM // 128, 128), F32)] * 3,
+        out_shape=[vmem(2 * TOK * DIM // 128, 128)] * 3,
         in_specs=[anywhere] * 8,
-        out_specs=[anywhere] * 3,
+        out_specs=[pl.BlockSpec(memory_space=pltpu.VMEM)] * 3,
         scratch_shapes=[
             vmem(2, TOK, DIM, dtype=BF16), vmem(2, TOK, DIM, dtype=BF16), vmem(2, TOK, DIM, dtype=BF16),
             vmem(2, 1, TOK), vmem(2, TOK, DIM, dtype=BF16), vmem(2, 3, DIM, DIM, dtype=BF16),
             *[vmem(2, TOK, DIM)] * 3, vmem(4, TOK, DIM),
             *[vmem(2, TOK, DIM, dtype=BF16)] * 4,
             *[vmem(TOK, DIM)] * 3,
-            *[vmem(TOK, DIM, dtype=BF16)] * 3,
+            *[vmem(TOK, DIM, dtype=BF16)] * 5,
             *[vmem(TOK, DIM)] * 3,
             *[vmem(TOK, DIM, dtype=BF16)] * 3,
             vmem(3, DIM, DIM),
@@ -497,22 +487,21 @@
             vmem(4, 3, 2, BAND, DIM, dtype=BF16),
             vmem(4, 3, 2, SIDE - 1, OWN, DIM, dtype=BF16),
             vmem(3, 3, DIM, DIM, dtype=BF16),
-            vmem(3, 2 * TOK * DIM // 128, 128),
-            sem((17,)), sem((3, 2)), sem((378,)), sem((378,)),
+            sem((17,)), sem((378,)), sem((378,)),
         ],
         compiler_params=pltpu.CompilerParams(
-            collective_id=0, has_side_effects=True, vmem_limit_bytes=60 * 2**20
+            collective_id=0, has_side_effects=True, vmem_limit_bytes=54 * 2**20
         ),
         cost_estimate=pl.CostEstimate(flops=7 * 10**9, bytes_accessed=9 * 10**6, transcendentals=10**6),
     )(*vectors, step_sizes.reshape(2, 1, TOK), out_grads.reshape(2, TOK, DIM), *matrices)
     result = pl.pallas_call(
         hand_out,
         out_shape=[jax.ShapeDtypeStruct((2 * TOK * DIM // 128, 128), F32)] * 3,
-        in_specs=[anywhere] * 3,
+        in_specs=[pl.BlockSpec(memory_space=pltpu.VMEM)] * 3,
         out_specs=[anywhere] * 3,
-        scratch_shapes=[vmem(3, 2 * TOK * DIM // 128, 128), sem((3, PARTS)), sem((3, PARTS))],
+        scratch_shapes=[sem((3, PARTS))],
         cost_estimate=pl.CostEstimate(flops=0, bytes_accessed=6 * 10**6, transcendentals=0),
-    )(*result)
+    )(*[pltpu.with_memory_space_constraint(part, pltpu.VMEM) for part in result])
     return tuple(part.reshape(2, TOK, 1, DIM) for part in result)
 
 

time: 96.8 us -> 92.1 us (0.951)
  Pallas kernels: 94.5 us -> 90.4 us
    pallas_call x1, Pallas kernels: 91.7 us -> 88.7 us  [local(): pl.pallas_call(kernel, out_shape=[vmem(2 * TOK * DIM // 128, 128)] * 3, i...]
    pallas_call x1, Pallas kernels: 2.81 us -> 1.76 us  [local(): pl.pallas_call(hand_out, out_shape=[jax.ShapeDtypeStruct((2 * TOK * DIM /...]
where the time goes in v3:
time: 92.1 us; the launch traced here: 91.2 us
  Pallas kernels  90.4 us (98%)
    pallas_call x1, Pallas kernels, local(): pl.pallas_call(kernel, out_shape=[vmem(2 * TOK * DIM // 128, 128)] * 3, i...  88.7 us

profile of v3, /device:TPU:2, one launch (start us, length us, event | category | flops | bytes accessed | tf_op | source)
XLA Modules:
  0.0 91.2 jit_solution(8680875127284404836)
XLA Ops:
  0.6 88.7 %shard_map.103 = (f32[2048,128]{1,0:T(8,128)S(1)}, f32[2048,128]{1,0:T(8,128)S(1)}, f32[2048,128]{1,0:T(8,128)S(1)}) custom-call(bf16[2,256,512]{2,1,0:T(8,128)(2,1)} %bitcast.17, bf16[2,256,512]{2,1,0:T(8,128)(2,1)} %bitcast.18, bf16[2,256,512]{2,1,0:T(8,128)(2,1)} %bitcast.19, f32[2,1,256]{2,1,0:T(1,128)} %bitcast.21, bf16[2,256,512]{2,1,0:T(8,128)(2,1)} %bitcast.20, ...), custom_call_target="tpu_custom_call" | custom-call | flops 7000000000 | bytes 9000000 | tf_op jit(solution)/shard_map/pallas_call | solution.py:466
  89.3 1.8 %shard_map.104 = (f32[2048,128]{1,0:T(8,128)}, f32[2048,128]{1,0:T(8,128)}, f32[2048,128]{1,0:T(8,128)}) custom-call(f32[2048,128]{1,0:T(8,128)S(1)} %get-tuple-element.9.query_ref, f32[2048,128]{1,0:T(8,128)S(1)} %get-tuple-element.10.key_ref, f32[2048,128]{1,0:T(8,128)S(1)} %get-tuple-element.11.value_ref), custom_call_target="tpu_custom_call" | custom-call | bytes 6000000 | tf_op jit(solution)/shard_map/pallas_call | solution.py:497

commit v4 on v3

--- a/solution.py
+++ b/solution.py
@@ -15,7 +15,6 @@
 HALF = DIM // 2
 BAND = HALF // SIDE
 OWN = BAND // SIDE
-PARTS = 4
 CHUNK = 16
 D_LATE, C_LATE, C_EARLY, D_EARLY = range(4)
 R_LATE, M_LATE, M_EARLY = range(3)
@@ -33,13 +32,44 @@
     return lax.dot_general(left, right, (((0,), (0,)), ((), ())), preferred_element_type=F32)
 
 
+def by_chunk(step):
+    def body(i, carry):
+        step(pl.ds(pl.multiple_of(i * CHUNK, CHUNK), CHUNK))
+        return carry
+
+    lax.fori_loop(0, TOK // CHUNK, body, 0, unroll=2)
+
+
+def hidden_of(first_back, third_back, factors, r):
+    return (first_back[r, :] * factors[1, r, :] + third_back[r, :] * factors[0, r, :]).astype(BF16)
+
+
+def lift_of(first_back, gated_back, factors, r):
+    return (first_back[r, :] * factors[2, r, :] + gated_back[r, :] * factors[0, r, :]).astype(BF16)
+
+
+def gate_of(first_back, third_back, gated_back, factors, r):
+    return (gated_back[r, :] * factors[1, r, :] + third_back[r, :] * factors[2, r, :]
+            + first_back[r, :] * factors[3, r, :]).astype(BF16)
+
+
+def spread(place, start, value):
+    for j in range(DIM // 128):
+        place[pl.ds(start * 4 + j, TOK, stride=4), :] = value[:, j * 128:(j + 1) * 128]
+
+
+def scaled(steps, total):
+    step = jnp.broadcast_to(steps, (128, TOK)).T
+    return jnp.concatenate([total[:, j * 128:(j + 1) * 128] * step for j in range(DIM // 128)], axis=1)
+
+
 def kernel(
     q_any, k_any, v_any, s_any, g_any, w1_any, w2_any, w3_any,
-    query_out, key_out, value_out,
-    q, k, v, s, g, w,
-    a_in, b_in, back, factors, gated, target, ga, gb,
+    query_out, key_out, value_out, key_part, value_part, first_back, third_back, gated_back, factors, w,
+    q, k, v, s, g,
+    a_in, b_in, back, gated, target, ga, gb,
     a_out, b_out, back_out, gated_out, ga_out, gb_out, ga_early, gb_early,
-    first_back, third_back, gated_back, gate_back, hidden_back, lift_back,
+    gate_back, hidden_back, lift_back,
     c_early, own_w, own_p, own_add, kept, summed,
     snd, passing, passed, got1, mid, got2, whole,
     in_sem, send_sem, recv_sem,
@@ -172,13 +202,6 @@
         for half in (0, 1):
             received(("ag3", c, m, half))
 
-    def by_chunk(step):
-        def body(i, carry):
-            step(rows(i * CHUNK, CHUNK))
-            return carry
-
-        lax.fori_loop(0, TOK // CHUNK, body, 0, unroll=2)
-
     def forward_inner(b):
         a_in[b] = nn(k[b], w[b, 0])
         b_in[b] = nn(k[b], w[b, 2])
@@ -268,27 +291,21 @@
 
         by_chunk(step)
 
-    def store_out(i, b, value):
-        place = (query_out, key_out, value_out)[i]
-        for j in range(DIM // 128):
-            place[pl.ds(b * TOK * 4 + j, TOK, stride=4), :] = value[:, j * 128:(j + 1) * 128]
-
     def hidden_step():
         def step(r):
-            hidden_back[r, :] = (first_back[r, :] * factors[1, r, :] + third_back[r, :] * factors[0, r, :]).astype(BF16)
+            hidden_back[r, :] = hidden_of(first_back, third_back, factors, r)
 
         by_chunk(step)
 
     def lift_step():
         def step(r):
-            lift_back[r, :] = (first_back[r, :] * factors[2, r, :] + gated_back[r, :] * factors[0, r, :]).astype(BF16)
+            lift_back[r, :] = lift_of(first_back, gated_back, factors, r)
 
         by_chunk(step)
 
     def gate_backward():
         def step(r):
-            gate_back[r, :] = (gated_back[r, :] * factors[1, r, :] + third_back[r, :] * factors[2, r, :]
-                               + first_back[r, :] * factors[3, r, :]).astype(BF16)
+            gate_back[r, :] = gate_of(first_back, third_back, gated_back, factors, r)
 
         by_chunk(step)
 
@@ -299,10 +316,6 @@
             gated_back[...] = nn(target[b], whole[c, 1])
         else:
             third_back[...] = nt(k[b], whole[c, 2])
-
-    def scaled(b, total):
-        step = jnp.broadcast_to(s[b], (128, TOK)).T
-        return jnp.concatenate([total[:, j * 128:(j + 1) * 128] * step for j in range(DIM // 128)], axis=1)
 
     def start_term(m):
         if m == 0:
@@ -383,7 +396,7 @@
     rs_relay(C_LATE, 2)
     each(rs_middle, C_LATE, (1, 0, 2))
     rs_relay(D_EARLY, 1)
-    store_out(0, 1, nn(ga_out[...], whole[R_LATE, 0]) + nn(gb_out[...], whole[R_LATE, 2]))
+    spread(query_out, TOK, nn(ga_out[...], whole[R_LATE, 0]) + nn(gb_out[...], whole[R_LATE, 2]))
     for m in (1, 0, 2):
         move, direct = renorm_back(1, m, rs_end(C_LATE, m))
         own_add[m] = move + direct
@@ -392,7 +405,7 @@
     rs_middle(D_EARLY, 2)
     update_factors(1)
     each(ag_middle, M_LATE, (1, 0, 2))
-    store_out(0, 0, nt(ga_early[...], w[1, 0]) + nt(gb_early[...], w[1, 2]))
+    spread(query_out, 0, nt(ga_early[...], w[1, 0]) + nt(gb_early[...], w[1, 2]))
     each(ag_relay, M_LATE, (1, 0, 2))
     rs_middle(D_EARLY, 1)
     ag_end(M_LATE, 1)
@@ -412,14 +425,14 @@
     rs_start(C_EARLY, 1)
     each(rs_relay, C_EARLY, (2, 0, 1))
     each(rs_middle, C_EARLY, (2, 0, 1))
-    store_out(1, 1, nn(ga[1], whole[M_LATE, 0]) + nn(gb[1], whole[M_LATE, 2])
-              + nt(gate_back[...], w[1, 0]) + nt(lift_back[...], w[1, 2]))
+    spread(key_out, 0, nn(ga[1], whole[M_LATE, 0]) + nn(gb[1], whole[M_LATE, 2])
+           + nt(gate_back[...], w[1, 0]) + nt(lift_back[...], w[1, 2]))
     for m in (0, 2, 1):
         own_update(0, m, rs_end(D_EARLY, m))
     for m in (2, 0, 1):
         move, _ = renorm_back(0, m, rs_end(C_EARLY, m) + own_add[m])
         ag_start(M_EARLY, m, move.astype(BF16))
-    store_out(2, 1, scaled(1, nt(gated[1], whole[M_LATE, 1]) + nn(hidden_back[...], w[1, 1])))
+    spread(value_out, 0, scaled(s[1], nt(gated[1], whole[M_LATE, 1]) + nn(hidden_back[...], w[1, 1])))
     each(ag_middle, M_EARLY, (2, 0, 1))
     update_factors(0)
     each(ag_relay, M_EARLY, (2, 0, 1))
@@ -427,29 +440,44 @@
     third_back[...] = nt(k[0], whole[M_EARLY, 2])
     ag_end(M_EARLY, 0)
     first_back[...] = nt(k[0], whole[M_EARLY, 0])
-    hidden_step()
-    key_part = nn(ga[0], whole[M_EARLY, 0]) + nn(gb[0], whole[M_EARLY, 2])
-    value_part = nn(hidden_back[...], w[0, 1])
+    key_part[...] = nn(ga[0], whole[M_EARLY, 0]) + nn(gb[0], whole[M_EARLY, 2])
     ag_end(M_EARLY, 1)
     gated_back[...] = nn(target[0], whole[M_EARLY, 1])
-    lift_step()
-    gate_backward()
-    store_out(1, 0, key_part + nt(gate_back[...], w[0, 0]) + nt(lift_back[...], w[0, 2]))
-    store_out(2, 0, scaled(0, value_part + nt(gated[0], whole[M_EARLY, 1])))
+    value_part[...] = nt(gated[0], whole[M_EARLY, 1])
     for copies in started.values():
         for copy in copies:
             copy.wait_send()
 
 
-def hand_out(query_ref, key_ref, value_ref, query_out, key_out, value_out, sems):
-    pairs = ((query_ref, query_out), (key_ref, key_out), (value_ref, value_out))
+def last_step(
+    steps, query_ref, key_ref, value_ref, key_part, value_part, first_back, third_back, gated_back, factors, w,
+    query_out, key_out, value_out,
+    gate_back, hidden_back, lift_back, key_last, value_last, sems,
+):
+    lines = key_ref.shape[0]
     copies = []
-    for i, (source, place) in enumerate(pairs):
-        for j in range(PARTS):
-            part = pl.ds(j * (source.shape[0] // PARTS), source.shape[0] // PARTS)
-            copies.append(pltpu.make_async_copy(source.at[part], place.at[part], sems.at[i, j]))
-    for copy in copies:
+
+    def leave(source, place):
+        copy = pltpu.make_async_copy(source, place, sems.at[len(copies)])
         copy.start()
+        copies.append(copy)
+
+    first, second = pl.ds(0, lines), pl.ds(lines, lines)
+    leave(query_ref.at[first], query_out.at[first])
+    leave(query_ref.at[second], query_out.at[second])
+    leave(key_ref, key_out.at[second])
+    leave(value_ref, value_out.at[second])
+
+    def step(r):
+        hidden_back[r, :] = hidden_of(first_back, third_back, factors, r)
+        lift_back[r, :] = lift_of(first_back, gated_back, factors, r)
+        gate_back[r, :] = gate_of(first_back, third_back, gated_back, factors, r)
+
+    by_chunk(step)
+    spread(key_last, 0, key_part[...] + nt(gate_back[...], w[0, 0]) + nt(lift_back[...], w[0, 2]))
+    leave(key_last, key_out.at[first])
+    spread(value_last, 0, scaled(steps[0], value_part[...] + nn(hidden_back[...], w[0, 1])))
+    leave(value_last, value_out.at[first])
     for copy in copies:
         copy.wait()
 
@@ -463,19 +491,20 @@
         return pltpu.VMEM(shape, dtype)
 
     sem = pltpu.SemaphoreType.DMA
+    lines = TOK * DIM // 128
     result = pl.pallas_call(
         kernel,
-        out_shape=[vmem(2 * TOK * DIM // 128, 128)] * 3,
+        out_shape=[vmem(2 * lines, 128), vmem(lines, 128), vmem(lines, 128), *[vmem(TOK, DIM)] * 5, vmem(4, TOK, DIM),
+                   vmem(2, 3, DIM, DIM, dtype=BF16)],
         in_specs=[anywhere] * 8,
-        out_specs=[pl.BlockSpec(memory_space=pltpu.VMEM)] * 3,
+        out_specs=[pl.BlockSpec(memory_space=pltpu.VMEM)] * 10,
         scratch_shapes=[
             vmem(2, TOK, DIM, dtype=BF16), vmem(2, TOK, DIM, dtype=BF16), vmem(2, TOK, DIM, dtype=BF16),
-            vmem(2, 1, TOK), vmem(2, TOK, DIM, dtype=BF16), vmem(2, 3, DIM, DIM, dtype=BF16),
-            *[vmem(2, TOK, DIM)] * 3, vmem(4, TOK, DIM),
+            vmem(2, 1, TOK), vmem(2, TOK, DIM, dtype=BF16),
+            *[vmem(2, TOK, DIM)] * 3,
             *[vmem(2, TOK, DIM, dtype=BF16)] * 4,
             *[vmem(TOK, DIM)] * 3,
             *[vmem(TOK, DIM, dtype=BF16)] * 5,
-            *[vmem(TOK, DIM)] * 3,
             *[vmem(TOK, DIM, dtype=BF16)] * 3,
             vmem(3, DIM, DIM),
             vmem(2, 3, 2 * OWN, DIM), vmem(2, 3, 2 * OWN, DIM), vmem(3, 2 * OWN, DIM),
@@ -490,18 +519,20 @@
             sem((17,)), sem((378,)), sem((378,)),
         ],
         compiler_params=pltpu.CompilerParams(
-            collective_id=0, has_side_effects=True, vmem_limit_bytes=54 * 2**20
+            collective_id=0, has_side_effects=True, vmem_limit_bytes=46 * 2**20
         ),
         cost_estimate=pl.CostEstimate(flops=7 * 10**9, bytes_accessed=9 * 10**6, transcendentals=10**6),
     )(*vectors, step_sizes.reshape(2, 1, TOK), out_grads.reshape(2, TOK, DIM), *matrices)
+    in_vmem = pl.BlockSpec(memory_space=pltpu.VMEM)
     result = pl.pallas_call(
-        hand_out,
-        out_shape=[jax.ShapeDtypeStruct((2 * TOK * DIM // 128, 128), F32)] * 3,
-        in_specs=[pl.BlockSpec(memory_space=pltpu.VMEM)] * 3,
+        last_step,
+        out_shape=[jax.ShapeDtypeStruct((2 * lines, 128), F32)] * 3,
+        in_specs=[in_vmem] * 11,
         out_specs=[anywhere] * 3,
-        scratch_shapes=[sem((3, PARTS))],
-        cost_estimate=pl.CostEstimate(flops=0, bytes_accessed=6 * 10**6, transcendentals=0),
-    )(*[pltpu.with_memory_space_constraint(part, pltpu.VMEM) for part in result])
+        scratch_shapes=[*[vmem(TOK, DIM, dtype=BF16)] * 3, *[vmem(lines, 128)] * 2, sem((6,))],
+        cost_estimate=pl.CostEstimate(flops=4 * 10**8, bytes_accessed=3 * 10**6, transcendentals=0),
+        compiler_params=pltpu.CompilerParams(vmem_limit_bytes=16 * 2**20),
+    )(step_sizes.reshape(2, 1, TOK), *[pltpu.with_memory_space_constraint(part, pltpu.VMEM) for part in result])
     return tuple(part.reshape(2, TOK, 1, DIM) for part in result)
 
 

time: 92.1 us -> 91.1 us (0.989)
  Pallas kernels: 90.4 us -> 89.4 us
    pallas_call x2, Pallas kernels: 90.4 us -> 89.4 us  [the longest x1 87.6 us: local(): pl.pallas_call(kernel, out_shape=[vmem(2 * lines, 128), vmem(lines, 128),...]
where the time goes in v4:
time: 91.1 us; the launch traced here: 90.2 us
  Pallas kernels  89.4 us (98%)
    pallas_call x1, Pallas kernels, local(): pl.pallas_call(kernel, out_shape=[vmem(2 * lines, 128), vmem(lines, 128),...  87.6 us

profile of v4, /device:TPU:2, one launch (start us, length us, event | category | flops | bytes accessed | tf_op | source)
XLA Modules:
  0.0 90.2 jit_solution(9001947108867233378)
XLA Ops:
  0.6 0.0 copy-start
  0.6 87.6 %shard_map.103 = (f32[2048,128]{1,0:T(8,128)S(1)}, f32[1024,128]{1,0:T(8,128)S(1)}, f32[1024,128]{1,0:T(8,128)S(1)}, f32[256,512]{1,0:T(8,128)S(1)}, f32[256,512...) custom-call(bf16[2,256,512]{2,1,0:T(8,128)(2,1)} %bitcast.19, ...), custom_call_target="tpu_custom_call" | custom-call | flops 7000000000 | bytes 9000000 | tf_op jit(solution)/shard_map/pallas_call | solution.py:495
  88.3 0.0 copy-done
  88.3 1.8 %shard_map.104 = (f32[2048,128]{1,0:T(8,128)}, f32[2048,128]{1,0:T(8,128)}, f32[2048,128]{1,0:T(8,128)}) custom-call(f32[2,1,256]{2,1,0:T(1,128)S(1)} %bitcast.12, f32[2048,128]{1,0:T(8,128)S(1)} %get-tuple-element.16.query_ref, f32[1024,128]{1,0:T(8,128)S(1)} %get-tuple-element.17.key_ref, f32[1024,128]{1,0:T(8,128)S(1)} %get-tuple-element.18.value_ref, ...), custom_call_target="tpu_custom_call" | custom-call | flops 400000000 | bytes 3000000 | tf_op jit(solution)/shard_map/pallas_call | solution.py:527
Async XLA Ops:
  0.6 87.6 %copy-start = (f32[2,256,1]{1,2,0:T(1,128)S(1)}, f32[2,256,1]{1,2,0:T(1,128)}, u32[]{:S(2)}) copy-start(f32[2,256,1]{1,2,0:T(1,128)} %param.11) | copy-start | bytes 6148
